TPU v7x, 32 devices: a whole 2x2x4 slice. The times are simulated.
32 devices in a mesh: dp: 2 (over x), ctx: 4 (over y, core), tp: 4 (over z).
Axes of the slice: x: 2, y: 2, z: 4, core: 2. Of those that a mesh axis runs over, the one named last changes fastest.
Arguments:
- tokens: bfloat16 [8, 2048, 768], P('dp', 'ctx'), may hold values from -6 to 6
- cotangent: bfloat16 [8, 2048, 768], P('dp', 'ctx'), may hold values from -6 to 6
- routes: int32 [8, 2048, 1], P('dp', 'ctx'), may hold values from 0 to 1; in each aligned block of 512 rows (0 to 511, 512 to 1023, ..., all dimensions but the last counted through in order) at most 384 rows name the same one
- qkv_weight: float32 [768, 3, 768], P('dp', None, 'tp'), may hold values from -0.21875 to 0.21875
- out_weight: float32 [768, 768], P('dp', 'tp'), may hold values from -3.5 to 3.5
- router_weight: float32 [768, 2], P('dp'), may hold values from -0.15625 to 0.15625
- bias_table: float32 [32, 12], P('dp', 'tp'), may hold values from -4 to 4
- norm_gains: float32 [768, 2], P('dp'), may hold values from 0.5 to 1.5
- expert_in: float32 [2, 768, 3072], P('dp', None, 'tp'), may hold values from -0.21875 to 0.21875
- expert_down: float32 [2, 3072, 768], P('dp', 'tp'), may hold values from -0.21875 to 0.21875
- qkv_first: float32 [768, 3, 768], P('dp', None, 'tp')
- qkv_second: float32 [768, 3, 768], P('dp', None, 'tp')
- out_first: float32 [768, 768], P('dp', 'tp')
- out_second: float32 [768, 768], P('dp', 'tp')
- router_first: float32 [768, 2], P('dp')
- router_second: float32 [768, 2], P('dp')
- table_first: float32 [32, 12], P('dp', 'tp')
- table_second: float32 [32, 12], P('dp', 'tp')
- gains_first: float32 [768, 2], P('dp')
- gains_second: float32 [768, 2], P('dp')
- in_first: float32 [2, 768, 3072], P('dp', None, 'tp')
- in_second: float32 [2, 768, 3072], P('dp', None, 'tp')
- down_first: float32 [2, 3072, 768], P('dp', 'tp')
- down_second: float32 [2, 3072, 768], P('dp', 'tp')
Outputs:
- mixed: bfloat16 [8, 2048, 768], P('dp', 'ctx')
- tokens_grad: float32 [8, 2048, 768], P('dp', 'ctx')
- query_key_value_first_moment_new: float32 [768, 3, 768], P('dp', None, 'tp')
- qkv_second_new: float32 [768, 3, 768], P('dp', None, 'tp')
- qkv_weight_new: float32 [768, 3, 768], P('dp', None, 'tp')
- out_first_new: float32 [768, 768], P('dp', 'tp')
- out_second_new: float32 [768, 768], P('dp', 'tp')
- out_weight_new: float32 [768, 768], P('dp', 'tp')
- router_first_new: float32 [768, 2], P('dp')
- router_second_new: float32 [768, 2], P('dp')
- router_weight_new: float32 [768, 2], P('dp')
- table_first_new: float32 [32, 12], P('dp', 'tp')
- table_second_new: float32 [32, 12], P('dp', 'tp')
- table_weight_new: float32 [32, 12], P('dp', 'tp')
- gains_first_new: float32 [768, 2], P('dp')
- gains_second_new: float32 [768, 2], P('dp')
- gains_weight_new: float32 [768, 2], P('dp')
- in_first_new: float32 [2, 768, 3072], P('dp', None, 'tp')
- in_second_new: float32 [2, 768, 3072], P('dp', None, 'tp')
- in_weight_new: float32 [2, 768, 3072], P('dp', None, 'tp')
- down_first_new: float32 [2, 3072, 768], P('dp', 'tp')
- down_second_new: float32 [2, 3072, 768], P('dp', 'tp')
- down_weight_new: float32 [2, 3072, 768], P('dp', 'tp')
Inputs may be any that keep to these rules, and one draw needn't show every extreme that they name: `routes`: in each block of 512 positions of a sequence (one device's tokens of it) no expert is named by more than 384 tokens, and some block reaches 384.
All inputs are finite; a program needn't handle non-finite values.
Results may differ from a plain program's by a relative error of at most 0.017.
The roundings to bfloat16 on the way count: a program that leaves them out, or rounds other values in their place, can miss the bound.
Values may be sent and summed in bfloat16 or wider, within the bound.
A program may use at most 320 MiB of HBM per device.

v0:
```python
from functools import partial

import jax
import jax.numpy as jnp
from jax import lax
from jax.sharding import PartitionSpec as P

D = 768
HEAD_DIM = 64
FF = 3072
LENGTH = 2048
STEP = 10


thresholds = (12, 16, 23, 32, 46, 64, 91)
beta_one = 0.9
beta_two = 0.999
epsilon = 1e-08
decay = 0.01


def bucket_of(query_pos, key_pos):
    offset = key_pos[None, :] - query_pos[:, None]
    distance = jnp.abs(offset)
    bucket = jnp.minimum(distance, 8)
    for border in thresholds:
        bucket = bucket + (distance >= border).astype(jnp.int32)
    return bucket + 16 * (offset > 0).astype(jnp.int32)


def rms_norm(values, gain_vector_row):
    return (
        values
        * lax.rsqrt(jnp.mean(values * values, axis=-1, keepdims=True) + 1e-06)
        * gain_vector_row
    )


def adamw(weight, gradient, moment_one, moment_two, step_rate):
    first_new = beta_one * moment_one + (1.0 - beta_one) * gradient
    second_new = beta_two * moment_two + (1.0 - beta_two) * gradient * gradient
    corrected_first = first_new / (1.0 - beta_one**STEP)
    corrected_second = second_new / (1.0 - beta_two**STEP)
    weight_new = weight - step_rate * (
        corrected_first / (jnp.sqrt(corrected_second) + epsilon) + decay * weight
    )
    return (first_new, second_new, weight_new)


def ctx_total(grad_qkv, grad_out, grad_router, grad_table, grad_gains, grad_in, grad_down):
    return lax.psum(
        (grad_qkv, grad_out, grad_router, grad_table, grad_gains, grad_in, grad_down), "ctx"
    )


def owner_total(grad_qkv, grad_out, grad_router, grad_table, grad_gains):
    return (
        lax.psum_scatter(grad_qkv, "dp", scatter_dimension=0, tiled=True),
        lax.psum_scatter(grad_out, "dp", scatter_dimension=0, tiled=True),
        lax.psum_scatter(grad_router, "dp", scatter_dimension=0, tiled=True),
        lax.psum_scatter(grad_table, "dp", scatter_dimension=0, tiled=True),
        lax.psum_scatter(grad_gains, "dp", scatter_dimension=0, tiled=True),
    )


def shards(
    tokens,
    cotangent,
    routes,
    qkv_weight,
    out_weight,
    router_weight,
    bias_table,
    norm_gains,
    expert_in,
    expert_down,
    qkv_first,
    qkv_second,
    out_first,
    out_second,
    router_first,
    router_second,
    table_first,
    table_second,
    gains_first,
    gains_second,
    in_first,
    in_second,
    down_first,
    down_second,
):
    seq_count, block_len, model_width = tokens.shape
    row_count = seq_count * block_len
    ctx_count = lax.axis_size("ctx")
    full_len = block_len * ctx_count
    ctx_place = lax.axis_index("ctx")
    w_qkv, w_out, w_router, bias_table_weight, w_gains = (
        lax.all_gather(qkv_weight.astype(jnp.bfloat16), "dp", axis=0, tiled=True),
        lax.all_gather(out_weight.astype(jnp.bfloat16), "dp", axis=0, tiled=True),
        lax.all_gather(router_weight.astype(jnp.bfloat16), "dp", axis=0, tiled=True),
        lax.all_gather(bias_table.astype(jnp.bfloat16), "dp", axis=0, tiled=True),
        lax.all_gather(norm_gains.astype(jnp.bfloat16), "dp", axis=0, tiled=True),
    )
    w_in = expert_in.astype(jnp.bfloat16)
    w_down = expert_down.astype(jnp.bfloat16)
    expert_count = w_router.shape[1]
    local_experts = expert_in.shape[0]
    dp_count = expert_count // local_experts
    heads_here = bias_table_weight.shape[1]
    bucket_count = bias_table_weight.shape[0]
    capacity = max(4, 3 * block_len // (2 * expert_count))
    score_scale = HEAD_DIM ** (-0.5)
    gain_one = w_gains[:, 0].astype(jnp.float32)
    gain_two = w_gains[:, 1].astype(jnp.float32)
    inputs = tokens.astype(jnp.float32).reshape(row_count, model_width)
    normed, norm_one_back = jax.vjp(rms_norm, inputs, gain_one)
    normed_low = normed.astype(jnp.bfloat16)
    projected = jnp.einsum(
        "rd,dtc->rtc", normed_low, w_qkv, preferred_element_type=jnp.float32
    ).astype(jnp.bfloat16)
    head_width = projected.shape[2]
    queries = projected[:, 0].reshape(seq_count, block_len, heads_here, HEAD_DIM)
    key_value = projected[:, 1:].reshape(seq_count, block_len, 2 * head_width)
    gathered_pairs = lax.all_gather(key_value, "ctx", axis=1, tiled=True)
    all_keys = gathered_pairs[..., :head_width].reshape(seq_count, full_len, heads_here, HEAD_DIM)
    all_values = gathered_pairs[..., head_width:].reshape(seq_count, full_len, heads_here, HEAD_DIM)
    query_pos = ctx_place * block_len + jnp.arange(block_len, dtype=jnp.int32)
    key_pos = jnp.arange(full_len, dtype=jnp.int32)
    buckets = bucket_of(query_pos, key_pos)
    bucket_onehot_matrix = (
        buckets[None, :, :] == jnp.arange(bucket_count, dtype=jnp.int32)[:, None, None]
    ).astype(jnp.bfloat16)
    relative_position_bias = jnp.einsum(
        "ayl,ar->ryl", bucket_onehot_matrix, bias_table_weight, preferred_element_type=jnp.float32
    )
    head_outs = []
    log_sums = []
    for seq_index in range(seq_count):
        scores = (
            jnp.einsum(
                "qhd,khd->hqk",
                queries[seq_index],
                all_keys[seq_index],
                preferred_element_type=jnp.float32,
            )
            * score_scale
            + relative_position_bias
        )
        top_score = jnp.max(scores, axis=-1, keepdims=True)
        log_total = top_score + jnp.log(
            jnp.sum(jnp.exp(scores - top_score), axis=-1, keepdims=True)
        )
        attend = jnp.exp(scores - log_total).astype(jnp.bfloat16)
        result_heads = jnp.einsum(
            "hqk,khd->qhd", attend, all_values[seq_index], preferred_element_type=jnp.float32
        )
        head_outs.append(result_heads.astype(jnp.bfloat16).reshape(block_len, head_width))
        log_sums.append(log_total)
    mixed_heads = jnp.stack(head_outs).reshape(row_count, head_width)
    attn_part = jnp.einsum("ri,ji->rj", mixed_heads, w_out, preferred_element_type=jnp.float32)
    attention = lax.psum(attn_part, "tp")
    hidden = inputs + attention
    normed_two, norm_two_back = jax.vjp(rms_norm, hidden, gain_two)
    normed_two_low = normed_two.astype(jnp.bfloat16)
    logits = jnp.dot(normed_two_low, w_router, preferred_element_type=jnp.float32)
    router_probs = jax.nn.softmax(logits, axis=-1)
    route_flat = routes.reshape(seq_count, block_len)
    route_hot = (
        route_flat[:, :, None] == jnp.arange(expert_count, dtype=jnp.int32)[None, None, :]
    ).astype(jnp.int32)
    earlier = jnp.cumsum(route_hot, axis=1) - route_hot
    slot_index = jnp.sum(earlier * route_hot, axis=-1)
    target = route_flat * capacity + slot_index
    route_mask = route_hot.reshape(row_count, expert_count).astype(jnp.float32)
    gate_value = jnp.sum(router_probs * route_mask, axis=-1)
    dispatch_hot = (
        target[:, None, :] == jnp.arange(expert_count * capacity, dtype=jnp.int32)[None, :, None]
    ).astype(jnp.bfloat16)
    outgoing = jnp.einsum(
        "sqt,std->sqd",
        dispatch_hot,
        normed_two_low.reshape(seq_count, block_len, model_width),
        preferred_element_type=jnp.float32,
    ).astype(jnp.bfloat16)
    outgoing = outgoing.reshape(seq_count, expert_count, capacity, model_width)
    arrived = lax.all_to_all(outgoing, "dp", split_axis=1, concat_axis=1, tiled=True).reshape(
        seq_count, dp_count, local_experts, capacity, model_width
    )
    pre_act = jnp.einsum("snemd,edf->snemf", arrived, w_in, preferred_element_type=jnp.float32)
    activated, gelu_back = jax.vjp(partial(jax.nn.gelu, approximate=True), pre_act)
    active_low = activated.astype(jnp.bfloat16)
    down_part = jnp.einsum(
        "snemf,efd->snemd", active_low, w_down, preferred_element_type=jnp.float32
    )
    down_slots = down_part.reshape(seq_count, expert_count, capacity, model_width)
    returned = lax.all_to_all(down_slots, "dp", split_axis=1, concat_axis=1, tiled=True)
    token_part = jnp.take_along_axis(
        returned.reshape(seq_count, expert_count * capacity, model_width),
        target[:, :, None],
        axis=1,
    )
    expert_rows = lax.psum(token_part.reshape(row_count, model_width), "tp")
    expert_rows = expert_rows.astype(jnp.bfloat16).astype(jnp.float32)
    mixed_out = (
        (hidden + gate_value[:, None] * expert_rows)
        .astype(jnp.bfloat16)
        .reshape(seq_count, block_len, model_width)
    )
    upstream = cotangent.astype(jnp.float32).reshape(row_count, model_width)
    gate_grad = jnp.sum(upstream * expert_rows, axis=-1)
    row_grad = (gate_value[:, None] * upstream).astype(jnp.bfloat16)
    grad_slots = jnp.einsum(
        "sqt,std->sqd",
        dispatch_hot,
        row_grad.reshape(seq_count, block_len, model_width),
        preferred_element_type=jnp.float32,
    ).astype(jnp.bfloat16)
    grad_arrived = lax.all_to_all(
        grad_slots.reshape(seq_count, expert_count, capacity, model_width),
        "dp",
        split_axis=1,
        concat_axis=1,
        tiled=True,
    )
    grad_arrived = grad_arrived.reshape(seq_count, dp_count, local_experts, capacity, model_width)
    act_grad = jnp.einsum(
        "snemd,efd->snemf", grad_arrived, w_down, preferred_element_type=jnp.float32
    )
    grad_down = jnp.einsum(
        "snemf,snemd->efd", active_low, grad_arrived, preferred_element_type=jnp.float32
    )
    pre_grad = gelu_back(act_grad)[0].astype(jnp.bfloat16)
    grad_in = jnp.einsum("snemd,snemf->edf", arrived, pre_grad, preferred_element_type=jnp.float32)
    slot_back = jnp.einsum("snemf,edf->snemd", pre_grad, w_in, preferred_element_type=jnp.float32)
    back_slots = slot_back.reshape(seq_count, expert_count, capacity, model_width)
    back_rows = lax.all_to_all(back_slots, "dp", split_axis=1, concat_axis=1, tiled=True)
    expert_backward_rows = jnp.take_along_axis(
        back_rows.reshape(seq_count, expert_count * capacity, model_width),
        target[:, :, None],
        axis=1,
    )
    expert_backward_rows = lax.psum(expert_backward_rows.reshape(row_count, model_width), "tp")
    prob_grad = route_mask * gate_grad[:, None]
    logit_grad = (
        router_probs * (prob_grad - jnp.sum(prob_grad * router_probs, axis=-1, keepdims=True))
    ).astype(jnp.bfloat16)
    grad_router = jnp.einsum(
        "rd,re->de", normed_two_low, logit_grad, preferred_element_type=jnp.float32
    )
    normed_two_grad = expert_backward_rows + jnp.einsum(
        "re,de->rd", logit_grad, w_router, preferred_element_type=jnp.float32
    )
    hidden_back, gain_two_grad = norm_two_back(normed_two_grad)
    hidden_grad = upstream + hidden_back
    hidden_low = hidden_grad.astype(jnp.bfloat16)
    grad_out = jnp.einsum("rj,ri->ji", hidden_low, mixed_heads, preferred_element_type=jnp.float32)
    heads_grad = jnp.einsum(
        "rj,ji->ri", hidden_low, w_out, preferred_element_type=jnp.float32
    ).astype(jnp.bfloat16)
    heads_grad = heads_grad.reshape(seq_count, block_len, heads_here, HEAD_DIM)
    query_grads = []
    pair_grads = []
    grad_table = jnp.zeros((bucket_count, heads_here), jnp.float32)
    for seq_index in range(seq_count):
        scores = (
            jnp.einsum(
                "qhd,khd->hqk",
                queries[seq_index],
                all_keys[seq_index],
                preferred_element_type=jnp.float32,
            )
            * score_scale
            + relative_position_bias
        )
        attend_full = jnp.exp(scores - log_sums[seq_index])
        attend = attend_full.astype(jnp.bfloat16)
        weight_grad = jnp.einsum(
            "qhd,khd->hqk",
            heads_grad[seq_index],
            all_values[seq_index],
            preferred_element_type=jnp.float32,
        )
        row_dot = jnp.sum(weight_grad * attend_full, axis=-1, keepdims=True)
        attention_score_grad = (attend_full * (weight_grad - row_dot)).astype(jnp.bfloat16)
        query_part = (
            jnp.einsum(
                "hqk,khd->qhd",
                attention_score_grad,
                all_keys[seq_index],
                preferred_element_type=jnp.float32,
            )
            * score_scale
        )
        query_grads.append(query_part.astype(jnp.bfloat16).reshape(block_len, head_width))
        key_part = (
            jnp.einsum(
                "hqk,qhd->khd",
                attention_score_grad,
                queries[seq_index],
                preferred_element_type=jnp.float32,
            )
            * score_scale
        )
        value_part = jnp.einsum(
            "hqk,qhd->khd", attend, heads_grad[seq_index], preferred_element_type=jnp.float32
        )
        pair_grads.append(
            jnp.concatenate(
                [key_part.reshape(full_len, head_width), value_part.reshape(full_len, head_width)],
                axis=-1,
            )
        )
        grad_table = grad_table + jnp.einsum(
            "xgz,egz->ex",
            attention_score_grad,
            bucket_onehot_matrix,
            preferred_element_type=jnp.float32,
        )
    pair_sum = lax.psum_scatter(
        jnp.stack(pair_grads), "ctx", scatter_dimension=1, tiled=True
    ).astype(jnp.bfloat16)
    projected_grad = jnp.concatenate(
        [
            jnp.stack(query_grads).reshape(row_count, 1, head_width),
            pair_sum.reshape(row_count, 2, head_width),
        ],
        axis=1,
    )
    grad_qkv = jnp.einsum(
        "rd,rtc->dtc", normed_low, projected_grad, preferred_element_type=jnp.float32
    )
    normed_grad = lax.psum(
        jnp.einsum("rtc,dtc->rd", projected_grad, w_qkv, preferred_element_type=jnp.float32), "tp"
    )
    input_back, gain_one_grad = norm_one_back(normed_grad)
    tokens_grad = (hidden_grad + input_back).reshape(seq_count, block_len, model_width)
    grad_gains = jnp.stack([gain_one_grad, gain_two_grad], axis=1)
    reduced_total = ctx_total(
        grad_qkv, grad_out, grad_router, grad_table, grad_gains, grad_in, grad_down
    )
    owned_grads = owner_total(
        reduced_total[0], reduced_total[1], reduced_total[2], reduced_total[3], reduced_total[4]
    )
    grad_in_total = reduced_total[5]
    grad_down_total = reduced_total[6]
    qkv_new = adamw(qkv_weight, owned_grads[0], qkv_first, qkv_second, 2.0 * D ** (-0.5))
    out_new = adamw(
        out_weight, owned_grads[1], out_first, out_second, 2.0 * max(1, 8 * D // LENGTH) ** (-0.5)
    )
    router_new = adamw(
        router_weight, owned_grads[2], router_first, router_second, 2.0 * (2 * D) ** (-0.5)
    )
    table_new = adamw(bias_table, owned_grads[3], table_first, table_second, 2.0)
    gains_new = adamw(norm_gains, owned_grads[4], gains_first, gains_second, 0.25)
    in_new = adamw(expert_in, grad_in_total, in_first, in_second, 2.0 * D ** (-0.5))
    down_new = adamw(
        expert_down,
        grad_down_total,
        down_first,
        down_second,
        2.0 * max(1, FF // (expert_count * expert_count)) ** (-0.5),
    )
    return (
        mixed_out,
        tokens_grad,
        qkv_new[0],
        qkv_new[1],
        qkv_new[2],
        out_new[0],
        out_new[1],
        out_new[2],
        router_new[0],
        router_new[1],
        router_new[2],
        table_new[0],
        table_new[1],
        table_new[2],
        gains_new[0],
        gains_new[1],
        gains_new[2],
        in_new[0],
        in_new[1],
        in_new[2],
        down_new[0],
        down_new[1],
        down_new[2],
    )


def solution(mesh):
    in_specs = (
        P("dp", "ctx", None),
        P("dp", "ctx", None),
        P("dp", "ctx", None),
        P("dp", None, "tp"),
        P("dp", "tp"),
        P("dp", None),
        P("dp", "tp"),
        P("dp", None),
        P("dp", None, "tp"),
        P("dp", "tp", None),
        P("dp", None, "tp"),
        P("dp", None, "tp"),
        P("dp", "tp"),
        P("dp", "tp"),
        P("dp", None),
        P("dp", None),
        P("dp", "tp"),
        P("dp", "tp"),
        P("dp", None),
        P("dp", None),
        P("dp", None, "tp"),
        P("dp", None, "tp"),
        P("dp", "tp", None),
        P("dp", "tp", None),
    )
    out_specs = (
        P("dp", "ctx", None),
        P("dp", "ctx", None),
        P("dp", None, "tp"),
        P("dp", None, "tp"),
        P("dp", None, "tp"),
        P("dp", "tp"),
        P("dp", "tp"),
        P("dp", "tp"),
        P("dp", None),
        P("dp", None),
        P("dp", None),
        P("dp", "tp"),
        P("dp", "tp"),
        P("dp", "tp"),
        P("dp", None),
        P("dp", None),
        P("dp", None),
        P("dp", None, "tp"),
        P("dp", None, "tp"),
        P("dp", None, "tp"),
        P("dp", "tp", None),
        P("dp", "tp", None),
        P("dp", "tp", None),
    )
    return jax.shard_map(shards, mesh=mesh, in_specs=in_specs, out_specs=out_specs, check_vma=False)
```

profile of v0, /device:TPU:0, one launch (start us, length us, event | category | flops | bytes accessed | tf_op | source)
XLA Modules:
  0.0 2029.8 jit_solution(6794487750110682618)
XLA Ops:
  17.9 11.8 all_gather.19
  62.2 22.2 %fusion.4 = f32[512,2048,3]{1,2,0:T(4,128)} fusion(bf16[32,3,1]{0,1,2:T(4,128)(2,1)S(1)} %reshape.427, s32[512,2048]{1,0:T(8,128)S(1)} %select_add_fusion), kind=kOutput, calls=%fused_computation.7 | convolution fusion | flops 234881024 | bytes 16777408 | tf_op jit(solution)/shard_map/ayl,ar->ryl/dot_general | solution.py:133
  95.3 14.8 fusion.174
  118.4 14.0 fusion.175
  140.4 14.4 fusion.176
  159.4 14.3 fusion.177
  181.2 6.8 fusion.110
  198.7 219.3 %all-reduce.8.cloned.1.call-done = f32[2048,768]{1,0:T(8,128)} async-done(((f32[2048,768]{1,0:T(8,128)}), f32[2048,768]{1,0:T(8,128)}) %all-reduce.8.cloned.1.call-update) | async-done | bytes 6291472 | tf_op jit(solution)/shard_map/psum | solution.py:161
  425.6 56.5 %all_to_all.20 = bf16[4,2,384,768]{3,2,0,1:T(8,128)(2,1)S(1)} all-to-all(bf16[4,2,384,768]{3,2,0,1:T(8,128)(2,1)S(1)} %copy.86), channel_id=1, replica_groups=mesh['dp'=2,'ctx'=4,'tp'=4] {'dp'}, dimensions={1} | all-to-all | bytes 9437184 | tf_op jit(solution)/shard_map/all_to_all | solution.py:186
  494.3 6.4 fusion.62
  500.7 7.4 all-to-all-start.1
  508.2 102.9 %all_gather.23 = bf16[768,2]{0,1:T(2,128)(2,1)S(1)} all-gather(bf16[384,2]{0,1:T(2,128)(2,1)S(1)} %convert_element_type.265), channel_id=1, replica_groups=mesh['dp'=2,'ctx'=4,'tp'=4] {'dp'}, dimensions={0}, use_global_device_ids=true | all-gather | bytes 4608 | tf_op jit(solution)/shard_map/all_gather | solution.py:100
  612.2 7.9 copy.89
  620.1 37.9 %gather_fusion = f32[2048,768]{1,0:T(8,128)} fusion(f32[4,768,768]{2,1,0:T(8,128)} %bitcast.321, s32[2048]{0:T(1024)S(1)} %bitcast.312), kind=kCustom, calls=%fused_computation.clone | custom fusion | bytes 12599296 | tf_op jit(solution)/shard_map/jit(take_along_axis)/gather | solution.py:197
  662.8 212.1 %all-reduce.15 = bf16[2048,768]{1,0:T(8,128)(2,1)S(1)} all-reduce(f32[2048,768]{1,0:T(8,128)} %bitcast.333), channel_id=1, replica_groups=mesh['dp'=2,'ctx'=4,'tp'=4] {'tp'}, use_global_device_ids=true, to_apply=%region_17.19 | all-reduce | flops 1572864 | bytes 9437184 | tf_op jit(solution)/shard_map/psum | solution.py:202
  882.8 51.7 %all_to_all.21 = bf16[4,2,384,768]{3,2,0,1:T(8,128)(2,1)S(1)} all-to-all(bf16[4,2,384,768]{3,2,0,1:T(8,128)(2,1)S(1)} %copy.90), channel_id=1, replica_groups=mesh['dp'=2,'ctx'=4,'tp'=4] {'dp'}, dimensions={1} | all-to-all | bytes 9437184 | tf_op jit(solution)/shard_map/all_to_all | solution.py:218
  934.6 10.0 fusion.48
  950.6 101.3 %all_to_all.22 = f32[4,2,384,768]{3,2,0,1:T(8,128)S(1)} all-to-all(f32[4,2,384,768]{3,2,0,1:T(8,128)S(1)} %fusion.64), channel_id=1, replica_groups=mesh['dp'=2,'ctx'=4,'tp'=4] {'dp'}, dimensions={1} | all-to-all | bytes 18874368 | tf_op jit(solution)/shard_map/all_to_all | solution.py:236
  1056.6 37.8 %gather_fusion.1 = f32[2048,768]{1,0:T(8,128)} fusion(f32[4,768,768]{2,1,0:T(8,128)} %bitcast.320, s32[2048]{0:T(1024)S(1)} %bitcast.313), kind=kCustom, calls=%fused_computation.1.clone | custom fusion | bytes 12599296 | tf_op jit(solution)/shard_map/jit(take_along_axis)/gather | solution.py:237
  1099.3 227.7 %all-reduce.10.cloned.1.call-done = f32[2048,768]{1,0:T(8,128)} async-done(((f32[2048,768]{1,0:T(8,128)}), f32[2048,768]{1,0:T(8,128)}) %all-reduce.10.cloned.1.call-update) | async-done | bytes 6291472 | tf_op jit(solution)/shard_map/psum | solution.py:242
  1327.0 6.7 multiply_reduce_fusion.4
  1333.7 6.3 fusion.32
  1343.2 8.2 fusion.92
  1351.5 6.6 multiply_reduce_fusion.2
  1366.9 8.0 fusion.96
  1374.9 10.8 multiply_reduce_fusion.3
  1395.2 12.1 multiply_convert_fusion.2
  1412.5 9.1 multiply_convert_fusion.1
  1426.8 12.5 multiply_convert_fusion.3
  1468.4 6.5 fusion.121
  1474.9 6.3 fusion.119
  1485.6 74.8 %reduce-scatter.13.cloned.1.call-done = f32[4,512,384]{1,2,0:T(8,128)} async-done(((f32[4,2048,384]{1,2,0:T(8,128)}), f32[4,512,384]{1,2,0:T(8,128)}) %reduce-scatter.13.cloned.1.call-update) | async-done | bytes 3145744 | tf_op jit(solution)/shard_map/reduce_scatter | solution.py:319
  1566.2 7.2 convolution_bitcast_fusion
  1579.0 6.5 fusion.182
  1587.4 9.2 fusion.81
  1596.6 24.1 %fusion.123 = f32[32,3]{0,1:T(4,128)S(1)} fusion(bf16[3,512,2048]{2,1,0:T(8,128)(2,1)} %multiply_convert_fusion.3, s32[512,2048]{1,0:T(8,128)S(1)} %copy-done.40), kind=kOutput, calls=%fused_computation.168 | convolution fusion | flops 234881024 | bytes 10486144 | tf_op jit(solution)/shard_map/xgz,egz->ex/dot_general | solution.py:313
  1620.7 22.6 %fusion.141 = f32[32,3]{0,1:T(4,128)S(1)} fusion(f32[32,3]{0,1:T(4,128)S(1)} %fusion.123, bf16[3,512,2048]{2,1,0:T(8,128)(2,1)S(1)} %bitcast.325, s32[512,2048]{1,0:T(8,128)S(1)} %copy-done.40), kind=kOutput, calls=%fused_computation.174 | convolution fusion | flops 234881120 | bytes 10486528 | tf_op jit(solution)/shard_map/xgz,egz->ex/dot_general | solution.py:313
  1643.3 22.8 %fusion.138 = f32[32,3]{0,1:T(4,128)S(1)} fusion(f32[32,3]{0,1:T(4,128)S(1)} %fusion.141, bf16[3,512,2048]{2,1,0:T(8,128)(2,1)S(1)} %bitcast.327, s32[512,2048]{1,0:T(8,128)S(1)} %copy-done.40), kind=kOutput, calls=%fused_computation.173 | convolution fusion | flops 234881120 | bytes 10486528 | tf_op jit(solution)/shard_map/xgz,egz->ex/dot_general | solution.py:313
  1666.1 23.6 %fusion.135 = f32[32,3]{0,1:T(4,128)S(1)} fusion(f32[32,3]{0,1:T(4,128)S(1)} %fusion.138, bf16[3,512,2048]{2,1,0:T(8,128)(2,1)} %multiply_convert_fusion, s32[512,2048]{1,0:T(8,128)S(1)} %copy-done.41), kind=kOutput, calls=%fused_computation.172 | convolution fusion | flops 234881120 | bytes 10486528 | tf_op jit(solution)/shard_map/xgz,egz->ex/dot_general | solution.py:313
  1690.5 105.9 %all-reduce.12.cloned.1.call-done = f32[2048,768]{1,0:T(8,128)} async-done(((f32[2048,768]{1,0:T(8,128)}), f32[2048,768]{1,0:T(8,128)}) %all-reduce.12.cloned.1.call-update) | async-done | bytes 6291472 | tf_op jit(solution)/shard_map/psum | solution.py:332
  1801.8 9.3 fusion.78
  1813.3 31.2 %reduce-scatter.15.cloned.1.call-done = f32[384,3,192]{0,2,1:T(8,128)} async-done(((f32[768,3,192]{0,2,1:T(8,128)}), f32[384,3,192]{0,2,1:T(8,128)}) %reduce-scatter.15.cloned.1.call-update) | async-done | bytes 884752 | tf_op jit(solution)/shard_map/reduce_scatter | solution.py:58
  1844.6 15.9 reduce-scatter.19.cloned.1.call-done
  1861.5 11.6 reduce-scatter.21.cloned.1.call-done
  1874.0 7.2 fusion.33
  1881.3 7.8 reduce-scatter.23.cloned.1.call-done
  1890.1 7.0 all-reduce
  1899.0 107.1 %all-reduce.14.cloned.1.call-done = (f32[384,3,192]{0,2,1:T(8,128)}, f32[384,192]{0,1:T(8,128)}, f32[1,768,768]{2,1,0:T(8,128)}, f32[1,768,768]{2,1,0:T(8,128)}) async-done(((f32[384,3,192]{0,2,1:T(8,128)}, f32[384,192]{0,1:T(8,128)}, f32[1,768,768]{2,1,0:T(8,128)}, f32[1,768,768]{2,1,0:T(8,128)}), (f32[384,3,192]{0,2,1:T(8,128)}, f32[384,192]{0,1:T(8,128)}, f32[1,768,768]{2,1,0:T(8,128)}, ...) | async-done | bytes 5898256 | tf_op jit(solution)/shard_map/psum | solution.py:51
  (389 shorter events, 250.2 us)
Async XLA Ops:
  7.2 22.5 %copy-start.6 = (bf16[4,512,768]{2,1,0:T(8,128)(2,1)S(1)}, bf16[4,512,768]{2,1,0:T(8,128)(2,1)}, u32[]{:S(2)}) copy-start(bf16[4,512,768]{2,1,0:T(8,128)(2,1)} %param.26) | copy-start | bytes 9437188
  7.2 83.2 %all-gather.3.cloned.1.call-start = ((), (), s32[]{:S(2)}) async-start(), calls=%async_computation.10 | async-start | bytes 7864320 | tf_op jit(solution)/shard_map/all_gather | solution.py:124
  13.5 19.0 copy-start.79
  42.4 375.7 %all-reduce.8.cloned.1.call-start = ((), (), s32[]{:S(2)}) async-start(), calls=%async_computation.11 | async-start | bytes 12582912 | tf_op jit(solution)/shard_map/psum | solution.py:161
  95.3 80.3 %copy-start.16 = (bf16[1,2048,192]{1,2,0:T(8,128)(2,1)}, bf16[1,2048,192]{1,2,0:T(8,128)(2,1)S(1)}, u32[]{:S(2)}) copy-start(bf16[1,2048,192]{1,2,0:T(8,128)(2,1)S(1)} %get-tuple-element.72) | copy-start | bytes 2359300
  159.4 21.8 %copy-start.72 = (f32[3,512]{1,0:T(4,128)}, f32[3,512]{1,0:T(4,128)S(1)}, u32[]{:S(2)}) copy-start(f32[3,512]{1,0:T(4,128)S(1)} %log_add_fusion.2) | copy-start | bytes 18436
  198.7 223.7 %copy-start.89 = (s32[4,512]{1,0:T(4,128)}, s32[4,512]{1,0:T(4,128)S(1)}, u32[]{:S(2)}) copy-start(s32[4,512]{1,0:T(4,128)S(1)} %multiply_add_fusion.4) | copy-start | bytes 24580
  422.3 188.8 %copy-start.8 = (bf16[2048,768]{1,0:T(8,128)(2,1)}, bf16[2048,768]{1,0:T(8,128)(2,1)S(1)}, u32[]{:S(2)}) copy-start(bf16[2048,768]{1,0:T(8,128)(2,1)S(1)} %multiply_convert_fusion.4) | copy-start | bytes 9437188
  425.5 58.6 %copy-start.43 = (f32[1,768,768]{2,1,0:T(8,128)S(1)}, f32[1,768,768]{2,1,0:T(8,128)}, u32[]{:S(2)}) copy-start(f32[1,768,768]{2,1,0:T(8,128)} %param.34) | copy-start | bytes 7077892
  500.7 111.5 %all-to-all-start.1 = ((f32[4,2,384,768]{3,2,0,1:T(8,128)}), f32[4,2,384,768]{3,2,0,1:T(8,128)}, u32[]{:S(2)}, u32[]{:S(2)}) async-start(f32[4,2,384,768]{3,2,0,1:T(8,128)} %fusion.62), calls=%async_computation.1 | async-start | bytes 18874368 | tf_op jit(solution)/shard_map/all_to_all | solution.py:196
  508.1 818.9 %all-reduce.10.cloned.1.call-start = ((), (), s32[]{:S(2)}) async-start(), calls=%async_computation.12 | async-start | bytes 12582912 | tf_op jit(solution)/shard_map/psum | solution.py:242
  611.1 46.8 %copy-start.83 = (pred[4,512]{1,0:T(4,128)(4,1)}, pred[4,512]{1,0:T(4,128)(4,1)S(1)}, u32[]{:S(2)}) copy-start(pred[4,512]{1,0:T(4,128)(4,1)S(1)} %and_bitcast_fusion) | copy-start | bytes 6148
  882.4 52.1 %slice-start.18 = ((s8[9437184]{0:T(1024)(128)(4,1)}), s8[4194304]{0:T(1024)(128)(4,1)S(1)}, s32[]{:S(2)}) async-start(s8[9437184]{0:T(1024)(128)(4,1)} %bitcast.337), calls=%async_computation.39 | async-start | bytes 8388608
  882.5 52.1 %slice-start.19 = ((s8[9437184]{0:T(1024)(128)(4,1)}), s8[4194304]{0:T(1024)(128)(4,1)S(1)}, s32[]{:S(2)}) async-start(s8[9437184]{0:T(1024)(128)(4,1)} %bitcast.337), calls=%async_computation.40 | async-start | bytes 8388608
  882.8 51.8 %slice-start.20 = ((s8[9437184]{0:T(1024)(128)(4,1)}), s8[1048576]{0:T(1024)(128)(4,1)S(1)}, s32[]{:S(2)}) async-start(s8[9437184]{0:T(1024)(128)(4,1)} %bitcast.337), calls=%async_computation.41 | async-start | bytes 2097152
  882.8 51.8 %copy-start.49 = (f32[1,768,768]{2,1,0:T(8,128)S(1)}, f32[1,768,768]{2,1,0:T(8,128)}, u32[]{:S(2)}) copy-start(f32[1,768,768]{2,1,0:T(8,128)} %param.35) | copy-start | bytes 7077892
  1056.6 37.8 %copy-start.84 = (pred[4,512]{1,0:T(4,128)(4,1)S(1)}, pred[4,512]{1,0:T(4,128)(4,1)}, u32[]{:S(2)}) copy-start(pred[4,512]{1,0:T(4,128)(4,1)} %copy-done.83) | copy-start | bytes 6148
  1099.2 461.2 %reduce-scatter.13.cloned.1.call-start = ((), (), s32[]{:S(2)}) async-start(), calls=%async_computation.13 | async-start | bytes 15728640 | tf_op jit(solution)/shard_map/reduce_scatter | solution.py:319
  1099.3 234.4 %copy-start.81 = (bf16[2048,2]{0,1:T(2,128)(2,1)}, bf16[2048,2]{0,1:T(2,128)(2,1)S(1)}, u32[]{:S(2)}) copy-start(bf16[2048,2]{0,1:T(2,128)(2,1)S(1)} %multiply_convert_fusion.5) | copy-start | bytes 24580
  1366.9 18.8 slice-start
  1462.3 334.1 %all-reduce.12.cloned.1.call-start = ((), (), s32[]{:S(2)}) async-start(), calls=%async_computation.14 | async-start | bytes 12582912 | tf_op jit(solution)/shard_map/psum | solution.py:332
  1573.4 239.9 %reduce-scatter.17.cloned.1.call-start = ((), (), s32[]{:S(2)}) async-start(), calls=%async_computation.16 | async-start | bytes 884736 | tf_op jit(solution)/shard_map/reduce_scatter | solution.py:59
  1578.9 265.7 %reduce-scatter.15.cloned.1.call-start = ((), (), s32[]{:S(2)}) async-start(), calls=%async_computation.15 | async-start | bytes 2654208 | tf_op jit(solution)/shard_map/reduce_scatter | solution.py:58
  1585.4 275.1 %reduce-scatter.19.cloned.1.call-start = ((), (), s32[]{:S(2)}) async-start(), calls=%async_computation.17 | async-start | bytes 589824
  1587.3 285.8 %reduce-scatter.21.cloned.1.call-start = ((), (), s32[]{:S(2)}) async-start(), calls=%async_computation.18 | async-start | bytes 24576
  1587.4 33.3 %slice-start.12 = ((s8[6291456]{0:T(1024)(128)(4,1)}), s8[4194304]{0:T(1024)(128)(4,1)S(1)}, s32[]{:S(2)}) async-start(s8[6291456]{0:T(1024)(128)(4,1)} %bitcast.324), calls=%async_computation.33 | async-start | bytes 8388608
  1596.6 24.1 %slice-start.13 = ((s8[6291456]{0:T(1024)(128)(4,1)}), s8[2097152]{0:T(1024)(128)(4,1)S(1)}, s32[]{:S(2)}) async-start(s8[6291456]{0:T(1024)(128)(4,1)} %bitcast.324), calls=%async_computation.34 | async-start | bytes 4194304
  1596.6 46.7 %slice-start.14 = ((s8[6291456]{0:T(1024)(128)(4,1)}), s8[4194304]{0:T(1024)(128)(4,1)S(1)}, s32[]{:S(2)}) async-start(s8[6291456]{0:T(1024)(128)(4,1)} %bitcast.326), calls=%async_computation.35 | async-start | bytes 8388608
  1620.7 22.6 %slice-start.15 = ((s8[6291456]{0:T(1024)(128)(4,1)}), s8[2097152]{0:T(1024)(128)(4,1)S(1)}, s32[]{:S(2)}) async-start(s8[6291456]{0:T(1024)(128)(4,1)} %bitcast.326), calls=%async_computation.36 | async-start | bytes 4194304
  1643.3 22.8 %copy-start.41 = (s32[512,2048]{1,0:T(8,128)S(1)}, s32[512,2048]{1,0:T(8,128)}, u32[]{:S(2)}) copy-start(s32[512,2048]{1,0:T(8,128)} %copy-done.39) | copy-start | bytes 12582916
  1666.1 23.7 %copy-start.85 = (f32[768]{0:T(1024)S(1)}, f32[768]{0:T(1024)}, u32[]{:S(2)}) copy-start(f32[768]{0:T(1024)} %get-tuple-element.24) | copy-start | bytes 9220
  1666.1 130.3 %copy-start.7 = (bf16[4,512,768]{2,1,0:T(8,128)(2,1)S(1)}, bf16[4,512,768]{2,1,0:T(8,128)(2,1)}, u32[]{:S(2)}) copy-start(bf16[4,512,768]{2,1,0:T(8,128)(2,1)} %param.26) | copy-start | bytes 9437188
  1666.1 130.3 %copy-start.76 = (f32[2048]{0:T(1024)S(1)}, f32[2048]{0:T(1024)}, u32[]{:S(2)}) copy-start(f32[2048]{0:T(1024)} %copy-done.75) | copy-start | bytes 24580
  1666.1 130.3 %copy-start.80 = (f32[768]{0:T(1024)S(1)}, f32[768]{0:T(1024)}, u32[]{:S(2)}) copy-start(f32[768]{0:T(1024)} %copy-done.79) | copy-start | bytes 9220
  1690.5 198.6 %reduce-scatter.23.cloned.1.call-start = ((), (), s32[]{:S(2)}) async-start(), calls=%async_computation.19 | async-start | bytes 589824
  1801.7 72.2 %copy-start.78 = (f32[1,4,4,128]{3,1,2,0:T(4,128)S(1)}, f32[1,4,4,128]{3,1,2,0:T(4,128)}, u32[]{:S(2)}) copy-start(f32[1,4,4,128]{3,1,2,0:T(4,128)} %copy-done.77) | copy-start | bytes 24580
  1801.7 204.3 %all-reduce.14.cloned.1.call-start = ((), (), s32[]{:S(2)}) async-start(), calls=%async_computation.20 | async-start | bytes 11796480 | tf_op jit(solution)/shard_map/psum | solution.py:51
  1873.9 23.2 %copy-start.91 = (f32[16,3]{0,1:T(4,128)S(1)}, f32[16,3]{0,1:T(4,128)}, u32[]{:S(2)}) copy-start(f32[16,3]{0,1:T(4,128)} %param.32) | copy-start | bytes 580
  1873.9 23.2 %copy-start.96 = (f32[16,3]{0,1:T(4,128)S(1)}, f32[16,3]{0,1:T(4,128)}, u32[]{:S(2)}) copy-start(f32[16,3]{0,1:T(4,128)} %param.43) | copy-start | bytes 580
  1873.9 23.2 %copy-start.97 = (f32[16,3]{0,1:T(4,128)S(1)}, f32[16,3]{0,1:T(4,128)}, u32[]{:S(2)}) copy-start(f32[16,3]{0,1:T(4,128)} %param.42) | copy-start | bytes 580
  1874.0 23.8 %copy-start.87 = (f32[384,2]{0,1:T(2,128)S(1)}, f32[384,2]{0,1:T(2,128)}, u32[]{:S(2)}) copy-start(f32[384,2]{0,1:T(2,128)} %param.31) | copy-start | bytes 9220
  1874.0 23.8 %copy-start.92 = (f32[384,2]{0,1:T(2,128)S(1)}, f32[384,2]{0,1:T(2,128)}, u32[]{:S(2)}) copy-start(f32[384,2]{0,1:T(2,128)} %param.41) | copy-start | bytes 9220
  1874.0 23.8 %copy-start.93 = (f32[384,2]{0,1:T(2,128)S(1)}, f32[384,2]{0,1:T(2,128)}, u32[]{:S(2)}) copy-start(f32[384,2]{0,1:T(2,128)} %param.40) | copy-start | bytes 9220
  1874.0 24.4 %copy-start.88 = (f32[384,2]{0,1:T(2,128)S(1)}, f32[384,2]{0,1:T(2,128)}, u32[]{:S(2)}) copy-start(f32[384,2]{0,1:T(2,128)} %param.33) | copy-start | bytes 9220
  1874.0 24.3 %copy-start.94 = (f32[384,2]{0,1:T(2,128)S(1)}, f32[384,2]{0,1:T(2,128)}, u32[]{:S(2)}) copy-start(f32[384,2]{0,1:T(2,128)} %param.45) | copy-start | bytes 9220
  1874.0 24.3 %copy-start.95 = (f32[384,2]{0,1:T(2,128)S(1)}, f32[384,2]{0,1:T(2,128)}, u32[]{:S(2)}) copy-start(f32[384,2]{0,1:T(2,128)} %param.44) | copy-start | bytes 9220
  1874.0 132.0 %copy-start.64 = (f32[384,192]{0,1:T(8,128)S(1)}, f32[384,192]{0,1:T(8,128)}, u32[]{:S(2)}) copy-start(f32[384,192]{0,1:T(8,128)} %param.30) | copy-start | bytes 884740
  1881.3 131.0 %copy-start.45 = (f32[1,768,768]{2,1,0:T(8,128)S(1)}, f32[1,768,768]{2,1,0:T(8,128)}, u32[]{:S(2)}) copy-start(f32[1,768,768]{2,1,0:T(8,128)} %param.34) | copy-start | bytes 7077892
  (83 other events, 593.7 us)
Sparse Core Ops, SparseCore 0:
  42.5 47.8 all-gather.2
  195.1 222.8 all-reduce.7
  1099.3 227.6 all-reduce.9
  1462.4 97.9 reduce-scatter.12
  1573.5 222.8 all-reduce.11
  1799.1 14.1 reduce-scatter.16
  1816.3 28.2 reduce-scatter.14
  1847.4 13.1 reduce-scatter.18
  1863.3 9.7 reduce-scatter.20
  1875.9 13.1 reduce-scatter.22
  1892.3 113.7 all-reduce.13
where the time goes:
time: 2040 us; the launch traced here: 2030 us
  waiting for transfers between devices  810 us (40%)
  blocking collectives  559 us (27%)
  matrix products  366 us (18%)
  local copies, waits for them, and re-layouts  145 us (7%)
  other arithmetic  127 us (6%)
    psum x1, waiting for transfers between devices, shards(): lax.psum(expert_backward_rows.reshape(row_count, model_width), 'tp')  228 us
    psum x1, waiting for transfers between devices, shards(): attention = lax.psum(attn_part, 'tp')  219 us
    psum x1, blocking collectives, shards(): expert_rows = lax.psum(token_part.reshape(row_count, model_width), 'tp')  212 us
    psum x1, waiting for transfers between devices, ctx_total(): lax.psum((grad_qkv, grad_out, grad_router, grad_table, grad_gains, grad_i...  107 us
    psum x1, waiting for transfers between devices, shards(): lax.psum(jnp.einsum('rtc,dtc->rd', projected_grad, w_qkv, preferred_eleme...  106 us
    all_gather x1, blocking collectives, shards(): lax.all_gather(router_weight.astype(jnp.bfloat16), 'dp', axis=0, tiled=True)  103 us
    all_to_all x1, blocking collectives, shards(): lax.all_to_all(back_slots, 'dp', split_axis=1, concat_axis=1, tiled=True)  101 us
    dot_general x4, matrix products, shards(): jnp.einsum('xgz,egz->ex', attention_score_grad, bucket_onehot_matrix, pre...  93.1 us
  transfers between devices with their start and end apart: 12, of which 11 were waited for; matrix products, arithmetic and copies ran while one was open for 10% of the time, Pallas kernels for 0%

commit v1 on v0

v1 whole, which is shorter than its diff:
```python
import jax
import jax.numpy as jnp
from jax import lax
from jax.experimental import pallas as pl
from jax.experimental.pallas import tpu as pltpu
from jax.sharding import PartitionSpec as P

D = 768
HEAD_DIM = 64
FF = 3072
LENGTH = 2048
STEP = 10
TILE = 256
BAND = 5


thresholds = (12, 16, 23, 32, 46, 64, 91)
beta_one = 0.9
beta_two = 0.999
epsilon = 1e-08
decay = 0.01


def bucket_of(query_pos, key_pos):
    offset = key_pos[:, None] - query_pos[None, :]
    distance = jnp.abs(offset)
    bucket = jnp.minimum(distance, 8)
    for border in thresholds:
        bucket = bucket + (distance >= border).astype(jnp.int32)
    return bucket + 16 * (offset > 0).astype(jnp.int32)


def rms_norm(values, gain_vector_row):
    return (
        values
        * lax.rsqrt(jnp.mean(values * values, axis=-1, keepdims=True) + 1e-06)
        * gain_vector_row
    )


def adamw(weight, gradient, moment_one, moment_two, step_rate):
    first_new = beta_one * moment_one + (1.0 - beta_one) * gradient
    second_new = beta_two * moment_two + (1.0 - beta_two) * gradient * gradient
    corrected_first = first_new / (1.0 - beta_one**STEP)
    corrected_second = second_new / (1.0 - beta_two**STEP)
    weight_new = weight - step_rate * (
        corrected_first / (jnp.sqrt(corrected_second) + epsilon) + decay * weight
    )
    return (first_new, second_new, weight_new)


def mm(a, b, dims):
    return lax.dot_general(a, b, (dims, ((), ())), preferred_element_type=jnp.float32)


def band_start(key_tile, query_tile):
    place = jnp.clip(key_tile - query_tile + BAND // 2, 0, BAND - 1)
    return pl.multiple_of(place * TILE, TILE)


def attend_forward(q_ref, k_ref, v_ref, bias_ref, out_ref, log_ref, scores):
    query_tile = lax.axis_index("ctx") * pl.num_programs(1) + pl.program_id(1)
    tiles = k_ref.shape[0] // TILE
    outs = []
    for head in range(2):
        cols = slice(head * HEAD_DIM, (head + 1) * HEAD_DIM)
        query = q_ref[:, cols] * HEAD_DIM ** (-0.5)
        top = None
        for tile in range(tiles):
            rows = slice(tile * TILE, (tile + 1) * TILE)
            score = mm(k_ref[rows, cols], query, ((1,), (1,)))
            score = score + bias_ref[head, pl.ds(band_start(tile, query_tile), TILE), :]
            scores[head, rows, :] = score
            high = jnp.max(score, axis=0, keepdims=True)
            top = high if top is None else jnp.maximum(top, high)
        total = jnp.zeros_like(top)
        result = jnp.zeros((HEAD_DIM, TILE), jnp.float32)
        for tile in range(tiles):
            rows = slice(tile * TILE, (tile + 1) * TILE)
            weight = jnp.exp(scores[head, rows, :] - top)
            total = total + jnp.sum(weight, axis=0, keepdims=True)
            result = result + mm(v_ref[rows, cols], weight.astype(jnp.bfloat16), ((0,), (0,)))
        outs.append(result / total)
        log_ref[0, pl.ds(head, 1), :] = top + jnp.log(total)
    out_ref[...] = jnp.concatenate(outs, axis=0).T.astype(jnp.bfloat16)


def attend_backward(
    q_ref, g_ref, k_ref, v_ref, bias_ref, log_ref,
    dq_ref, dk_ref, dv_ref, band_ref,
    weights, changes, key_sum, value_sum,
):
    step = pl.program_id(1)
    last = pl.num_programs(1) - 1
    query_tile = lax.axis_index("ctx") * pl.num_programs(1) + step
    tiles = k_ref.shape[0] // TILE

    @pl.when(step == 0)
    def _():
        key_sum[...] = jnp.zeros_like(key_sum)
        value_sum[...] = jnp.zeros_like(value_sum)
        band_ref[...] = jnp.zeros_like(band_ref)

    query_parts = []
    for head in range(2):
        cols = slice(head * HEAD_DIM, (head + 1) * HEAD_DIM)
        query = q_ref[:, cols] * HEAD_DIM ** (-0.5)
        grad = g_ref[:, cols]
        log_total = log_ref[0, pl.ds(head, 1), :]
        row_dot = jnp.zeros_like(log_total)
        for tile in range(tiles):
            rows = slice(tile * TILE, (tile + 1) * TILE)
            start = band_start(tile, query_tile)
            score = mm(k_ref[rows, cols], query, ((1,), (1,)))
            score = score + bias_ref[head, pl.ds(start, TILE), :]
            weight = jnp.exp(score - log_total)
            change = mm(v_ref[rows, cols], grad, ((1,), (1,)))
            row_dot = row_dot + jnp.sum(weight * change, axis=0, keepdims=True)
            weights[head, rows, :] = weight
            changes[head, rows, :] = change
            value_sum[head, rows, :] += mm(weight.astype(jnp.bfloat16), grad, ((1,), (0,)))
        part = jnp.zeros((HEAD_DIM, TILE), jnp.float32)
        for tile in range(tiles):
            rows = slice(tile * TILE, (tile + 1) * TILE)
            start = band_start(tile, query_tile)
            slope = weights[head, rows, :] * (changes[head, rows, :] - row_dot)
            low = slope.astype(jnp.bfloat16)
            band_ref[head, pl.ds(start, TILE), :] += low.astype(jnp.float32)
            part = part + mm(k_ref[rows, cols], low, ((0,), (0,)))
            key_sum[head, rows, :] += mm(low, query, ((1,), (0,)))
        query_parts.append(part)
    query_grad = jnp.concatenate(query_parts, axis=0).T * HEAD_DIM ** (-0.5)
    dq_ref[...] = query_grad.astype(jnp.bfloat16)

    @pl.when(step == last)
    def _():
        dk_ref[...] = jnp.concatenate([key_sum[0], key_sum[1]], axis=1).astype(jnp.bfloat16)
        dv_ref[...] = jnp.concatenate([value_sum[0], value_sum[1]], axis=1).astype(jnp.bfloat16)


def attention_specs(block_len, full_len, pairs):
    query = pl.BlockSpec((TILE, 2 * HEAD_DIM), lambda p, i: (i, p))
    key = pl.BlockSpec((full_len, 2 * HEAD_DIM), lambda p, i: (0, p))
    value = pl.BlockSpec((full_len, 2 * HEAD_DIM), lambda p, i: (0, p + pairs))
    bias = pl.BlockSpec((2, BAND * TILE, TILE), lambda p, i: (p, 0, 0))
    logs = pl.BlockSpec((1, 2, TILE), lambda p, i: (p, 0, i))
    return query, key, value, bias, logs


def run_forward(queries, key_value, bias):
    block_len, width = queries.shape
    full_len = key_value.shape[0]
    pairs = width // (2 * HEAD_DIM)
    query, key, value, strip, logs = attention_specs(block_len, full_len, pairs)
    return pl.pallas_call(
        attend_forward,
        grid=(pairs, block_len // TILE),
        in_specs=[query, key, value, strip],
        out_specs=[query, logs],
        out_shape=[
            jax.ShapeDtypeStruct((block_len, width), jnp.bfloat16),
            jax.ShapeDtypeStruct((pairs, 2, block_len), jnp.float32),
        ],
        scratch_shapes=[pltpu.VMEM((2, full_len, TILE), jnp.float32)],
        compiler_params=pltpu.CompilerParams(vmem_limit_bytes=40 * 2**20),
        cost_estimate=pl.CostEstimate(
            flops=16 * block_len * full_len * width,
            bytes_accessed=20 * 2**20,
            transcendentals=block_len * full_len * width // HEAD_DIM,
        ),
    )(queries, key_value, key_value, bias)


def run_backward(queries, grads, key_value, bias, log_sums):
    block_len, width = queries.shape
    full_len = key_value.shape[0]
    pairs = width // (2 * HEAD_DIM)
    query, key, value, strip, logs = attention_specs(block_len, full_len, pairs)
    whole = jax.ShapeDtypeStruct((full_len, width), jnp.bfloat16)
    return pl.pallas_call(
        attend_backward,
        grid=(pairs, block_len // TILE),
        in_specs=[query, query, key, value, strip, logs],
        out_specs=[query, key, key, strip],
        out_shape=[
            jax.ShapeDtypeStruct((block_len, width), jnp.bfloat16),
            whole,
            whole,
            jax.ShapeDtypeStruct((2 * pairs, BAND * TILE, TILE), jnp.float32),
        ],
        scratch_shapes=[
            pltpu.VMEM((2, full_len, TILE), jnp.float32),
            pltpu.VMEM((2, full_len, TILE), jnp.float32),
            pltpu.VMEM((2, full_len, HEAD_DIM), jnp.float32),
            pltpu.VMEM((2, full_len, HEAD_DIM), jnp.float32),
        ],
        compiler_params=pltpu.CompilerParams(vmem_limit_bytes=48 * 2**20),
        cost_estimate=pl.CostEstimate(
            flops=40 * block_len * full_len * width,
            bytes_accessed=40 * 2**20,
            transcendentals=block_len * full_len * width // HEAD_DIM,
        ),
    )(queries, grads, key_value, key_value, bias, log_sums)


def shards(
    tokens,
    cotangent,
    routes,
    qkv_weight,
    out_weight,
    router_weight,
    bias_table,
    norm_gains,
    expert_in,
    expert_down,
    qkv_first,
    qkv_second,
    out_first,
    out_second,
    router_first,
    router_second,
    table_first,
    table_second,
    gains_first,
    gains_second,
    in_first,
    in_second,
    down_first,
    down_second,
):
    seq_count, block_len, model_width = tokens.shape
    tp_count = lax.axis_size("tp")
    dp_count = lax.axis_size("dp")
    tp_place = lax.axis_index("tp")
    assert seq_count == tp_count and expert_in.shape[0] == 1
    full_len = block_len * lax.axis_size("ctx")
    local_rows, _, local_width = qkv_weight.shape
    expert_count = router_weight.shape[1]
    table_rows, local_heads = bias_table.shape
    bucket_count = table_rows * dp_count
    head_count = local_heads * tp_count
    capacity = max(4, 3 * block_len // (2 * expert_count))
    low = jnp.bfloat16

    small_sizes = (local_rows * expert_count, local_rows * 2, table_rows * local_heads)
    small_count = sum(small_sizes)
    small_rows = -(-small_count // model_width)

    def pack_small(router, gains, table):
        flat = jnp.concatenate([router.reshape(-1), gains.reshape(-1), table.reshape(-1)])
        flat = jnp.pad(flat, (0, small_rows * model_width - small_count))
        return flat.reshape(small_rows, model_width)

    def cut_small(flat):
        ends = (small_sizes[0], small_sizes[0] + small_sizes[1])
        return flat[..., : ends[0]], flat[..., ends[0] : ends[1]], flat[..., ends[1] : small_count]

    main = jnp.concatenate([qkv_weight, out_weight[:, None, :]], axis=1)
    main = jnp.transpose(main, (1, 2, 0)).astype(low).reshape(4 * local_width, local_rows)
    shared = lax.all_gather(main, ("dp", "tp"), axis=0)
    small = lax.all_gather(
        pack_small(router_weight.astype(low), norm_gains.astype(low), bias_table.astype(low)),
        ("dp", "tp"),
        axis=0,
    )
    in_rows = lax.all_gather(expert_in[0].T.astype(low), "tp", axis=0, tiled=True)
    down_rows = lax.all_gather(expert_down[0].astype(low), "tp", axis=0, tiled=True)

    shared = shared.reshape(dp_count, tp_count, 4, local_width, local_rows)
    shared = jnp.transpose(shared, (2, 1, 3, 0, 4)).reshape(4 * model_width, model_width)
    w_qkv = shared[: 3 * model_width]
    w_out = shared[3 * model_width :]
    small = small.reshape(dp_count, tp_count, -1)
    router_flat, gains_flat, table_flat = cut_small(small)
    w_router = router_flat[:, 0].reshape(model_width, expert_count)
    w_gains = gains_flat[:, 0].reshape(model_width, 2)
    w_table = jnp.transpose(
        table_flat.reshape(dp_count, tp_count, table_rows, local_heads), (0, 2, 1, 3)
    ).reshape(bucket_count, head_count)
    gain_one = w_gains[:, 0].astype(jnp.float32)
    gain_two = w_gains[:, 1].astype(jnp.float32)

    strip_keys = jnp.arange(BAND * TILE, dtype=jnp.int32)
    strip_queries = jnp.arange(TILE, dtype=jnp.int32) + (BAND // 2) * TILE
    strip_buckets = bucket_of(strip_queries, strip_keys)
    strip_hot = (
        strip_buckets[None] == jnp.arange(bucket_count, dtype=jnp.int32)[:, None, None]
    ).astype(low)
    bias = jnp.einsum("bh,bkq->hkq", w_table, strip_hot, preferred_element_type=jnp.float32)

    own = lax.dynamic_index_in_dim(tokens, tp_place, 0, keepdims=False)
    inputs = own.astype(jnp.float32)
    normed, norm_one_back = jax.vjp(rms_norm, inputs, gain_one)
    normed_low = normed.astype(low)
    key_value_here = jnp.einsum(
        "rd,cd->rc", normed_low, w_qkv[model_width:], preferred_element_type=jnp.float32
    ).astype(low)
    key_value = lax.all_gather(key_value_here, "ctx", axis=0, tiled=True)
    queries = jnp.einsum(
        "rd,cd->rc", normed_low, w_qkv[:model_width], preferred_element_type=jnp.float32
    ).astype(low)
    mixed_heads, log_sums = run_forward(queries, key_value, bias)
    attention = jnp.einsum("rc,co->ro", mixed_heads, w_out, preferred_element_type=jnp.float32)
    hidden = inputs + attention
    normed_two, norm_two_back = jax.vjp(rms_norm, hidden, gain_two)
    normed_two_low = normed_two.astype(low)
    logits = jnp.dot(normed_two_low, w_router, preferred_element_type=jnp.float32)
    router_probs = jax.nn.softmax(logits, axis=-1)
    route_flat = lax.dynamic_index_in_dim(routes, tp_place, 0, keepdims=False)[:, 0]
    route_hot = (
        route_flat[:, None] == jnp.arange(expert_count, dtype=jnp.int32)[None, :]
    ).astype(jnp.int32)
    earlier = jnp.cumsum(route_hot, axis=0) - route_hot
    slot_index = jnp.sum(earlier * route_hot, axis=-1)
    target = route_flat * capacity + slot_index
    route_mask = route_hot.astype(jnp.float32)
    gate_value = jnp.sum(router_probs * route_mask, axis=-1)
    dispatch_hot = (
        target[None, :] == jnp.arange(expert_count * capacity, dtype=jnp.int32)[:, None]
    ).astype(low)

    def to_experts(rows):
        slots = jnp.dot(dispatch_hot, rows, preferred_element_type=jnp.float32).astype(low)
        return lax.all_to_all(slots, "dp", split_axis=0, concat_axis=0, tiled=True)

    def from_experts(slots):
        back = lax.all_to_all(slots.astype(low), "dp", split_axis=0, concat_axis=0, tiled=True)
        return jnp.einsum("tr,td->rd", dispatch_hot, back, preferred_element_type=jnp.float32)

    upstream = lax.dynamic_index_in_dim(cotangent, tp_place, 0, keepdims=False)
    upstream = upstream.astype(jnp.float32)
    row_grad = (gate_value[:, None] * upstream).astype(low)
    arrived = to_experts(normed_two_low)
    grad_arrived = to_experts(row_grad)
    pre_act = jnp.einsum("md,fd->mf", arrived, in_rows, preferred_element_type=jnp.float32)
    activated, gelu_back = jax.vjp(lambda a: jax.nn.gelu(a, approximate=True), pre_act)
    active_low = activated.astype(low)
    down_slots = jnp.dot(active_low, down_rows, preferred_element_type=jnp.float32)
    expert_rows = from_experts(down_slots)
    act_grad = jnp.einsum("md,fd->mf", grad_arrived, down_rows, preferred_element_type=jnp.float32)
    pre_grad = gelu_back(act_grad)[0].astype(low)
    slot_back = jnp.dot(pre_grad, in_rows, preferred_element_type=jnp.float32)
    expert_backward_rows = from_experts(slot_back)
    grad_down = jnp.einsum(
        "mf,md->fd", active_low, grad_arrived, preferred_element_type=jnp.float32
    ).astype(low)
    grad_in = jnp.einsum(
        "mf,md->fd", pre_grad, arrived, preferred_element_type=jnp.float32
    ).astype(low)
    grad_down = lax.psum_scatter(grad_down, "tp", scatter_dimension=0, tiled=True)
    grad_in = lax.psum_scatter(grad_in, "tp", scatter_dimension=0, tiled=True)
    grad_down, grad_in = lax.psum((grad_down, grad_in), "ctx")

    mixed_here = (hidden + gate_value[:, None] * expert_rows).astype(low)
    mixed_out = lax.all_gather(mixed_here, "tp", axis=0)
    gate_grad = jnp.sum(upstream * expert_rows, axis=-1)
    prob_grad = route_mask * gate_grad[:, None]
    logit_grad = (
        router_probs * (prob_grad - jnp.sum(prob_grad * router_probs, axis=-1, keepdims=True))
    ).astype(low)
    grad_router = jnp.einsum(
        "rd,re->de", normed_two_low, logit_grad, preferred_element_type=jnp.float32
    )
    normed_two_grad = expert_backward_rows + jnp.einsum(
        "re,de->rd", logit_grad, w_router, preferred_element_type=jnp.float32
    )
    hidden_back, gain_two_grad = norm_two_back(normed_two_grad)
    hidden_grad = upstream + hidden_back
    hidden_low = hidden_grad.astype(low)
    grad_out = jnp.einsum("rc,ro->co", mixed_heads, hidden_low, preferred_element_type=jnp.float32)
    heads_grad = jnp.einsum(
        "ro,co->rc", hidden_low, w_out, preferred_element_type=jnp.float32
    ).astype(low)
    query_grad, key_grad, value_grad, strip_grad = run_backward(
        queries, heads_grad, key_value, bias, log_sums
    )
    key_grad = lax.psum_scatter(key_grad, "ctx", scatter_dimension=0, tiled=True)
    value_grad = lax.psum_scatter(value_grad, "ctx", scatter_dimension=0, tiled=True)
    grad_table = jnp.einsum(
        "hkq,bkq->bh", strip_grad, strip_hot, preferred_element_type=jnp.float32
    )
    projected_grad = jnp.concatenate([query_grad, key_grad, value_grad], axis=1)
    grad_qkv = jnp.einsum(
        "rc,rd->cd", projected_grad, normed_low, preferred_element_type=jnp.float32
    )
    normed_grad = jnp.einsum(
        "rc,cd->rd", projected_grad, w_qkv, preferred_element_type=jnp.float32
    )
    input_back, gain_one_grad = norm_one_back(normed_grad)
    tokens_grad = lax.all_gather((hidden_grad + input_back).astype(low), "tp", axis=0)
    tokens_grad = tokens_grad.astype(jnp.float32)
    grad_gains = jnp.stack([gain_one_grad, gain_two_grad], axis=1)

    main_grad = jnp.concatenate([grad_qkv, grad_out], axis=0).astype(low)
    main_grad = main_grad.reshape(4, tp_count, local_width, dp_count, local_rows)
    main_grad = jnp.transpose(main_grad, (3, 1, 0, 2, 4)).reshape(-1, local_rows)
    main_grad = lax.psum_scatter(main_grad, ("dp", "tp"), scatter_dimension=0, tiled=True)
    main_grad = lax.psum(main_grad, "ctx").reshape(4, local_width, local_rows)
    main_grad = jnp.transpose(main_grad, (2, 0, 1)).astype(jnp.float32)
    small_grad = lax.psum(
        jnp.concatenate([grad_router.reshape(-1), grad_gains.reshape(-1), grad_table.reshape(-1)]),
        ("dp", "ctx", "tp"),
    )
    dp_place = lax.axis_index("dp")
    ends = (model_width * expert_count, model_width * (expert_count + 2))
    router_total = small_grad[: ends[0]].reshape(model_width, expert_count)
    gains_total = small_grad[ends[0] : ends[1]].reshape(model_width, 2)
    table_total = small_grad[ends[1] :].reshape(bucket_count, head_count)
    router_total = lax.dynamic_slice_in_dim(router_total, dp_place * local_rows, local_rows, 0)
    gains_total = lax.dynamic_slice_in_dim(gains_total, dp_place * local_rows, local_rows, 0)
    table_total = lax.dynamic_slice(
        table_total,
        (dp_place * table_rows, tp_place * local_heads),
        (table_rows, local_heads),
    )

    qkv_new = adamw(qkv_weight, main_grad[:, :3], qkv_first, qkv_second, 2.0 * D ** (-0.5))
    out_new = adamw(
        out_weight, main_grad[:, 3], out_first, out_second, 2.0 * max(1, 8 * D // LENGTH) ** (-0.5)
    )
    router_new = adamw(
        router_weight, router_total, router_first, router_second, 2.0 * (2 * D) ** (-0.5)
    )
    table_new = adamw(bias_table, table_total, table_first, table_second, 2.0)
    gains_new = adamw(norm_gains, gains_total, gains_first, gains_second, 0.25)
    in_new = adamw(
        expert_in,
        grad_in.T[None].astype(jnp.float32),
        in_first,
        in_second,
        2.0 * D ** (-0.5),
    )
    down_new = adamw(
        expert_down,
        grad_down[None].astype(jnp.float32),
        down_first,
        down_second,
        2.0 * max(1, FF // (expert_count * expert_count)) ** (-0.5),
    )
    return (
        mixed_out,
        tokens_grad,
        *qkv_new,
        *out_new,
        *router_new,
        *table_new,
        *gains_new,
        *in_new,
        *down_new,
    )


def solution(mesh):
    in_specs = (
        P("dp", "ctx", None),
        P("dp", "ctx", None),
        P("dp", "ctx", None),
        P("dp", None, "tp"),
        P("dp", "tp"),
        P("dp", None),
        P("dp", "tp"),
        P("dp", None),
        P("dp", None, "tp"),
        P("dp", "tp", None),
        P("dp", None, "tp"),
        P("dp", None, "tp"),
        P("dp", "tp"),
        P("dp", "tp"),
        P("dp", None),
        P("dp", None),
        P("dp", "tp"),
        P("dp", "tp"),
        P("dp", None),
        P("dp", None),
        P("dp", None, "tp"),
        P("dp", None, "tp"),
        P("dp", "tp", None),
        P("dp", "tp", None),
    )
    out_specs = (
        P("dp", "ctx", None),
        P("dp", "ctx", None),
        P("dp", None, "tp"),
        P("dp", None, "tp"),
        P("dp", None, "tp"),
        P("dp", "tp"),
        P("dp", "tp"),
        P("dp", "tp"),
        P("dp", None),
        P("dp", None),
        P("dp", None),
        P("dp", "tp"),
        P("dp", "tp"),
        P("dp", "tp"),
        P("dp", None),
        P("dp", None),
        P("dp", None),
        P("dp", None, "tp"),
        P("dp", None, "tp"),
        P("dp", None, "tp"),
        P("dp", "tp", None),
        P("dp", "tp", None),
        P("dp", "tp", None),
    )
    return jax.shard_map(shards, mesh=mesh, in_specs=in_specs, out_specs=out_specs, check_vma=False)
```

time: 2040 us -> 1080 us (0.53)
  blocking collectives: 559 us -> 91.3 us
  matrix products: 366 us -> 116 us
  waiting for transfers between devices: 810 us -> 604 us
  Pallas kernels: 0 us -> 95.1 us
  other arithmetic: 127 us -> 39.1 us
  local copies, waits for them, and re-layouts: 145 us -> 100 us
    psum x4 -> x1, waiting for transfers between devices: 660 us -> 61.5 us  [shards(): main_grad = lax.psum(main_grad, 'ctx').reshape(4, local_width, local_rows)]
    all_gather x1 -> x6, waiting for transfers between devices: 6.02 us -> 240 us  [the longest x1 79.3 us: shards(): lax.all_gather(expert_down[0].astype(low), 'tp', axis=0, tiled=True)]
    dot_general x41 -> x20, matrix products: 348 us -> 114 us  [the longest x1 20.3 us: shards(): jnp.einsum('hkq,bkq->bh', strip_grad, strip_hot, preferred_element_type=j...]
    all_to_all x3 -> x1, blocking collectives: 210 us -> 17.2 us  [to_experts(): return lax.all_to_all(slots, 'dp', split_axis=0, concat_axis=0, tiled=True)]
    psum x2 -> x1, blocking collectives: 219 us -> 41.4 us  [shards(): lax.psum(jnp.concatenate([grad_router.reshape(-1), grad_gains.reshape(-1)...]
    reduce_scatter x3 -> x5, waiting for transfers between devices: 108 us -> 274 us  [the longest x1 100 us: shards(): lax.psum_scatter(main_grad, ('dp', 'tp'), scatter_dimension=0, tiled=True)]
    all_gather x5 -> x1, blocking collectives: 130 us -> 32.6 us  [shards(): lax.all_gather(pack_small(router_weight.astype(low), norm_gains.astype(lo...]
    pallas_call x0 -> x2, Pallas kernels: none -> 95.1 us  [the longest x1 62.5 us: run_backward(): pl.pallas_call(attend_backward, grid=(pairs, block_len // TILE), in_specs...]
  transfers between devices with their start and end apart: 12 -> 15, of which waited for: 11 -> 14; matrix products, arithmetic and copies ran while one was open for 10% -> 15% of each run, Pallas kernels for 0% -> 3%
where the time goes in v1:
time: 1080 us
  waiting for transfers between devices  604 us (56%)
  matrix products  116 us (11%)
  local copies, waits for them, and re-layouts  100 us (9%)
  Pallas kernels  95.1 us (9%)
  blocking collectives  91.3 us (8%)
  other arithmetic  39.1 us (4%)
  starting transfers between devices  15.2 us (1%)
  between operations  15.2 us (1%)
    reduce_scatter x1, waiting for transfers between devices, shards(): lax.psum_scatter(main_grad, ('dp', 'tp'), scatter_dimension=0, tiled=True)  100 us
    reduce_scatter x1, waiting for transfers between devices, shards(): grad_in = lax.psum_scatter(grad_in, 'tp', scatter_dimension=0, tiled=True)  88.1 us
    all_gather x1, waiting for transfers between devices, shards(): lax.all_gather(expert_down[0].astype(low), 'tp', axis=0, tiled=True)  79.3 us
    pallas_call x1, Pallas kernels, run_backward(): pl.pallas_call(attend_backward, grid=(pairs, block_len // TILE), in_specs...  62.5 us
    psum x1, waiting for transfers between devices, shards(): main_grad = lax.psum(main_grad, 'ctx').reshape(4, local_width, local_rows)  61.5 us
    all_gather x1, waiting for transfers between devices, shards(): shared = lax.all_gather(main, ('dp', 'tp'), axis=0)  47.7 us
    all_gather x1, waiting for transfers between devices, shards(): lax.all_gather(expert_in[0].T.astype(low), 'tp', axis=0, tiled=True)  46.7 us
    unnamed x118, local copies, waits for them, and re-layouts  46.2 us
  transfers between devices with their start and end apart: 15, of which 14 were waited for; matrix products, arithmetic and copies ran while one was open for 15% of the time, Pallas kernels for 3%

profile of v1, /device:TPU:0, one launch (start us, length us, event | category | flops | bytes accessed | tf_op | source)
XLA Modules:
  0.0 1076.6 jit_solution(16602081183056701100)
XLA Ops:
  11.5 32.6 %all_gather.27 = bf16[8,3,768]{2,1,0:T(4,128)(2,1)S(1)} all-gather(bf16[1,3,768]{2,1,0:T(4,128)(2,1)S(1)} %all_gather_reshape.6), channel_id=1, replica_groups=mesh['dp'=2,'ctx'=4,'tp'=4] {'dp','tp'}, dimensions={0}, use_global_device_ids=true | all-gather | bytes 41472 | tf_op jit(solution)/shard_map/all_gather | solution.py:262
  46.2 47.7 %all-gather.10.cloned.1.call-done = bf16[8,768,384]{2,1,0:T(8,128)(2,1)} async-done(((bf16[1,768,384]{2,1,0:T(8,128)(2,1)}), bf16[8,768,384]{2,1,0:T(8,128)(2,1)}) %all-gather.10.cloned.1.call-update) | async-done | bytes 4718608 | tf_op jit(solution)/shard_map/all_gather | solution.py:261
  98.9 3.9 convolution_convert_fusion.3
  104.1 2.8 convert_element_type.261
  108.6 10.6 fusion.1
  119.2 17.6 %copy.257.bias_ref = f32[12,1280,256]{2,1,0:T(8,128)} copy(f32[12,1280,256]{2,0,1:T(8,128)} %fusion.1) | data formatting | bytes 31457280 | tf_op jit(solution)/shard_map/bh,bkq->hkq/dot_general | solution.py:290
  147.5 2.8 copy-done.2
  150.3 32.6 %shard_map.407 = (bf16[512,768]{1,0:T(8,128)(2,1)S(1)}, f32[6,2,512]{2,1,0:T(2,128)S(1)}) custom-call(bf16[512,768]{1,0:T(8,128)(2,1)S(1)} %convolution_convert_fusion.7.q_ref, bf16[2048,1536]{1,0:T(8,128)(2,1)S(1)} %copy-done.2, bf16[2048,1536]{1,0:T(8,128)(2,1)S(1)} %copy-done.2, f32[12,1280,256]{2,1,0:T(8,128)} %copy.257.bias_ref), custom_call_target="tpu_custom_call" | custom-call | flops 12884901888 | bytes 20971520 | tf_op jit(solution)/shard_map/pallas_call | solution.py:155
  187.9 4.5 all-to-all-start
  192.4 46.7 %all-gather.14.cloned.1.call-done = bf16[3072,768]{0,1:T(8,128)(2,1)} async-done(((bf16[768,768]{0,1:T(8,128)(2,1)}), bf16[3072,768]{0,1:T(8,128)(2,1)}) %all-gather.14.cloned.1.call-update) | async-done | bytes 4718608 | tf_op jit(solution)/shard_map/all_gather | solution.py:267
  239.1 10.6 fusion.123
  249.7 79.3 %all-gather.16.cloned.1.call-done = bf16[1,3072,768]{2,1,0:T(8,128)(2,1)} async-done(((bf16[1,768,768]{2,1,0:T(8,128)(2,1)}), bf16[1,3072,768]{2,1,0:T(8,128)(2,1)}) %all-gather.16.cloned.1.call-update) | async-done | bytes 4718608 | tf_op jit(solution)/shard_map/all_gather | solution.py:268
  329.0 11.5 %fusion.49 = bf16[768,768]{1,0:T(8,128)(2,1)} fusion(bf16[1,3072,768]{2,1,0:T(8,128)(2,1)} %all-gather.16.cloned.1.call-done, f32[768,3072]{1,0:T(8,128)} %fusion.123), kind=kOutput, calls=%fused_computation.75 | convolution fusion | flops 3645702144 | bytes 15335424 | tf_op jit(solution)/shard_map/dot_general | solution.py:339
  340.5 4.6 all-to-all-start.1
  347.1 13.5 %all-to-all-done.1 = bf16[2,384,768]{2,1,0:T(8,128)(2,1)} async-done(((bf16[2,384,768]{2,1,0:T(8,128)(2,1)}), bf16[2,384,768]{2,1,0:T(8,128)(2,1)}, u32[]{:S(2)}, u32[]{:S(2)}) %all-to-all-start.1) | async-done | bytes 1179680 | tf_op jit(solution)/shard_map/all_to_all | solution.py:328
  360.6 3.7 fusion.42
  366.5 17.2 %all_to_all.48 = bf16[2,384,768]{2,1,0:T(8,128)(2,1)S(1)} all-to-all(bf16[2,384,768]{2,1,0:T(8,128)(2,1)S(1)} %bitcast.188), channel_id=1, replica_groups=mesh['dp'=2,'ctx'=4,'tp'=4] {'dp'}, dimensions={0} | all-to-all | bytes 2359296 | tf_op jit(solution)/shard_map/all_to_all | solution.py:325
  383.8 10.8 %fusion.11 = bf16[768,3072]{1,0:T(8,128)(2,1)S(1)} fusion(f32[768,3072]{1,0:T(8,128)S(1)} %copy-done.44, bf16[768,768]{1,0:T(8,128)(2,1)S(1)} %bitcast.182, bf16[1,3072,768]{2,1,0:T(8,128)(2,1)} %all-gather.16.cloned.1.call-done), kind=kOutput, calls=%fused_computation.14 | convolution fusion | flops 3671064576 | bytes 20054016 | tf_op jit(solution)/shard_map/md,fd->mf/dot_general | solution.py:341
  394.7 4.9 convolution_convert_fusion.5
  399.5 4.5 all-to-all-start.3
  404.3 13.4 %all-to-all-done.3 = bf16[2,384,768]{2,1,0:T(8,128)(2,1)} async-done(((bf16[2,384,768]{2,1,0:T(8,128)(2,1)}), bf16[2,384,768]{2,1,0:T(8,128)(2,1)}, u32[]{:S(2)}, u32[]{:S(2)}) %all-to-all-start.3) | async-done | bytes 1179680 | tf_op jit(solution)/shard_map/all_to_all | solution.py:328
  421.3 2.7 convert_add_fusion
  425.1 62.5 %shard_map.408 = (bf16[512,768]{1,0:T(8,128)(2,1)S(1)}, bf16[2048,768]{1,0:T(8,128)(2,1)}, bf16[2048,768]{1,0:T(8,128)(2,1)}, f32[12,1280,256]{2,1,0:T(8,128)}) custom-call(bf16[512,768]{1,0:T(8,128)(2,1)S(1)} %convolution_convert_fusion.7.q_ref, bf16[512,768]{1,0:T(8,128)(2,1)S(1)} %convolution_convert_fusion.6.g_ref, ...), custom_call_target="tpu_custom_call" | custom-call | flops 32212254720 | bytes 41943040 | tf_op jit(solution)/shard_map/pallas_call | solution.py:180
  488.3 8.7 convolution_convert_fusion
  497.3 8.7 convolution_convert_fusion.1
  509.3 14.4 %reduce-scatter.6.cloned.1.call-done = bf16[512,768]{1,0:T(8,128)(2,1)} async-done(((bf16[2048,768]{1,0:T(8,128)(2,1)}), bf16[512,768]{1,0:T(8,128)(2,1)}) %reduce-scatter.6.cloned.1.call-update) | async-done | bytes 786448 | tf_op jit(solution)/shard_map/reduce_scatter | solution.py:378
  525.7 38.4 %reduce-scatter.8.cloned.1.call-done = bf16[512,768]{1,0:T(8,128)(2,1)} async-done(((bf16[2048,768]{1,0:T(8,128)(2,1)}), bf16[512,768]{1,0:T(8,128)(2,1)}) %reduce-scatter.8.cloned.1.call-update) | async-done | bytes 786448 | tf_op jit(solution)/shard_map/reduce_scatter | solution.py:379
  566.2 4.0 convolution_convert_fusion.2
  570.2 2.5 pad_maximum_fusion
  572.7 10.3 convert_element_type.277
  582.9 5.5 copy.261
  592.0 3.6 copy.260
  604.4 3.2 copy.277
  609.6 3.2 copy.270
  614.8 3.1 copy.275
  618.5 33.2 %reduce-scatter.14.cloned.1.call-done = bf16[768,768]{0,1:T(8,128)(2,1)} async-done(((bf16[3072,768]{0,1:T(8,128)(2,1)}), bf16[768,768]{0,1:T(8,128)(2,1)}) %reduce-scatter.14.cloned.1.call-update) | async-done | bytes 1179664 | tf_op jit(solution)/shard_map/reduce_scatter | solution.py:351
  651.8 88.1 %reduce-scatter.12.cloned.1.call-done = bf16[768,768]{1,0:T(8,128)(2,1)} async-done(((bf16[3072,768]{1,0:T(8,128)(2,1)}), bf16[768,768]{1,0:T(8,128)(2,1)}) %reduce-scatter.12.cloned.1.call-update) | async-done | bytes 1179664 | tf_op jit(solution)/shard_map/reduce_scatter | solution.py:352
  739.9 100.1 %reduce-scatter.10.cloned.1.call-done = bf16[768,384]{1,0:T(8,128)(2,1)} async-done(((bf16[6144,384]{1,0:T(8,128)(2,1)}), bf16[768,384]{1,0:T(8,128)(2,1)}) %reduce-scatter.10.cloned.1.call-update) | async-done | bytes 589840 | tf_op jit(solution)/shard_map/reduce_scatter | solution.py:398
  840.0 20.3 %fusion.61 = f32[32,12]{1,0:T(8,128)S(1)} fusion(f32[12,1280,256]{2,1,0:T(8,128)} %get-tuple-element.34, s32[1280,256]{1,0:T(8,128)S(1)} %copy-done.14), kind=kOutput, calls=%fused_computation.94 | convolution fusion | flops 262144000 | bytes 17040896 | tf_op jit(solution)/shard_map/hkq,bkq->bh/dot_general | solution.py:380
  860.5 44.7 %all-gather.18.cloned.1.call-done = bf16[2048,768]{1,0:T(8,128)(2,1)} async-done(((bf16[512,768]{1,0:T(8,128)(2,1)}), bf16[2048,768]{1,0:T(8,128)(2,1)}) %all-gather.18.cloned.1.call-update) | async-done | bytes 3145744 | tf_op jit(solution)/shard_map/all_gather | solution.py:356
  905.7 41.4 %psum.29 = f32[3456]{0:T(1024)S(1)} all-reduce(f32[3456]{0:T(1024)S(1)} %pad_maximum_fusion.2), channel_id=1, replica_groups=mesh['dp'=2,'ctx'=4,'tp'=4] {'dp','ctx','tp'}, use_global_device_ids=true, to_apply=%region_18.19 | all-reduce | flops 3456 | bytes 27648 | tf_op jit(solution)/shard_map/psum | solution.py:401
  950.2 20.3 %all-gather.20.cloned.1.call-done = bf16[2048,768]{1,0:T(8,128)(2,1)} async-done(((bf16[512,768]{1,0:T(8,128)(2,1)}), bf16[2048,768]{1,0:T(8,128)(2,1)}) %all-gather.20.cloned.1.call-update) | async-done | bytes 3145744 | tf_op jit(solution)/shard_map/all_gather | solution.py:391
  970.5 5.3 convert.25
  975.8 61.5 %all-reduce.4.cloned.1.call-done = (bf16[384,4,192]{0,2,1:T(8,128)(2,1)}, bf16[768,768]{0,1:T(8,128)(2,1)}, bf16[768,768]{0,1:T(8,128)(2,1)}) async-done(((bf16[384,4,192]{0,2,1:T(8,128)(2,1)}, bf16[768,768]{0,1:T(8,128)(2,1)}, bf16[768,768]{0,1:T(8,128)(2,1)}), (bf16[384,4,192]{0,2,1:T(8,128)(2,1)}, bf16[768,768]{0,1:T(8,128)(2,1)}, bf16[768,768]{0,1:T(8,128)(2,1)})) %all-reduce.4.cloned.1.call-update) | async-done | bytes 2949136 | tf_op jit(solution)/shard_map/psum | solution.py:399
  1037.4 10.0 multiply_subtract_fusion
  1047.4 3.2 copy.278
  1052.5 3.2 copy.280
  1057.7 3.2 copy.282
  (221 shorter events, 79.9 us)
Async XLA Ops:
  7.2 129.6 %copy-start = (s32[4,512,1]{1,2,0:T(1,128)S(1)}, s32[4,512,1]{1,2,0:T(1,128)}, u32[]{:S(2)}) copy-start(s32[4,512,1]{1,2,0:T(1,128)} %param.26) | copy-start | bytes 24580
  7.2 3.3 copy-start.32
  7.2 3.6 copy-start.34
  7.2 4.0 copy-start.36
  7.2 86.7 %all-gather.10.cloned.1.call-start = ((), (), s32[]{:S(2)}) async-start(), calls=%async_computation.9 | async-start | bytes 5308416 | tf_op jit(solution)/shard_map/all_gather | solution.py:261
  10.4 137.1 %all-gather.12.cloned.1.call-start = ((), (), s32[]{:S(2)}) async-start(), calls=%async_computation.10 | async-start | bytes 7864320 | tf_op jit(solution)/shard_map/all_gather | solution.py:299
  45.9 50.0 %copy-start.30 = (f32[512]{0:T(512)}, f32[512]{0:T(512)S(1)}, u32[]{:S(2)}) copy-start(f32[512]{0:T(512)S(1)} %fusion.35) | copy-start | bytes 6148
  98.9 4.0 copy-start.5
  102.8 136.3 %all-gather.14.cloned.1.call-start = ((), (), s32[]{:S(2)}) async-start(), calls=%async_computation.11 | async-start | bytes 5898240 | tf_op jit(solution)/shard_map/all_gather | solution.py:267
  104.0 225.0 %all-gather.16.cloned.1.call-start = ((), (), s32[]{:S(2)}) async-start(), calls=%async_computation.17 | async-start | bytes 5898240 | tf_op jit(solution)/shard_map/all_gather | solution.py:268
  108.5 10.6 copy-start.13
  147.5 2.8 copy-start.2
  150.3 32.7 %copy-start.20 = (bf16[96,8,2,384]{3,1,2,0:T(8,128)(2,1)S(1)}, bf16[96,8,2,384]{3,1,2,0:T(8,128)(2,1)}, u32[]{:S(2)}) copy-start(bf16[96,8,2,384]{3,1,2,0:T(8,128)(2,1)} %copy.293) | copy-start | bytes 3538948
  187.9 51.2 %all-to-all-start = ((bf16[2,384,768]{2,1,0:T(8,128)(2,1)}), bf16[2,384,768]{2,1,0:T(8,128)(2,1)}, u32[]{:S(2)}, u32[]{:S(2)}) async-start(bf16[2,384,768]{2,1,0:T(8,128)(2,1)} %bitcast.186), calls=%async_computation | async-start | bytes 2359296 | tf_op jit(solution)/shard_map/all_to_all | solution.py:325
  340.5 20.1 %all-to-all-start.1 = ((bf16[2,384,768]{2,1,0:T(8,128)(2,1)}), bf16[2,384,768]{2,1,0:T(8,128)(2,1)}, u32[]{:S(2)}, u32[]{:S(2)}) async-start(bf16[2,384,768]{2,1,0:T(8,128)(2,1)} %bitcast.185), calls=%async_computation.1 | async-start | bytes 2359296 | tf_op jit(solution)/shard_map/all_to_all | solution.py:328
  360.6 23.2 %copy-start.44 = (f32[768,3072]{1,0:T(8,128)S(1)}, f32[768,3072]{1,0:T(8,128)}, u32[]{:S(2)}) copy-start(f32[768,3072]{1,0:T(8,128)} %fusion.123) | copy-start | bytes 28311556
  366.5 28.1 %slice-start = ((s8[4718592]{0:T(1024)(128)(4,1)}), s8[4194304]{0:T(1024)(128)(4,1)S(1)}, s32[]{:S(2)}) async-start(s8[4718592]{0:T(1024)(128)(4,1)} %bitcast.198), calls=%async_computation.21 | async-start | bytes 8388608
  383.8 10.9 %copy-start.22 = (bf16[2,384,768]{2,1,0:T(8,128)(2,1)}, bf16[2,384,768]{2,1,0:T(8,128)(2,1)S(1)}, u32[]{:S(2)}) copy-start(bf16[2,384,768]{2,1,0:T(8,128)(2,1)S(1)} %all_to_all.48) | copy-start | bytes 3538948
  383.8 10.9 %slice-start.1 = ((s8[4718592]{0:T(1024)(128)(4,1)}), s8[524288]{0:T(1024)(128)(4,1)S(1)}, s32[]{:S(2)}) async-start(s8[4718592]{0:T(1024)(128)(4,1)} %bitcast.198), calls=%async_computation.22 | async-start | bytes 1048576
  394.7 4.9 copy-start.45
  399.5 18.1 %all-to-all-start.3 = ((bf16[2,384,768]{2,1,0:T(8,128)(2,1)}), bf16[2,384,768]{2,1,0:T(8,128)(2,1)}, u32[]{:S(2)}, u32[]{:S(2)}) async-start(bf16[2,384,768]{2,1,0:T(8,128)(2,1)} %bitcast.184), calls=%async_computation.3 | async-start | bytes 2359296 | tf_op jit(solution)/shard_map/all_to_all | solution.py:328
  404.0 119.6 %reduce-scatter.6.cloned.1.call-start = ((), (), s32[]{:S(2)}) async-start(), calls=%async_computation.12 | async-start | bytes 3932160 | tf_op jit(solution)/shard_map/reduce_scatter | solution.py:378
  487.7 76.5 %reduce-scatter.8.cloned.1.call-start = ((), (), s32[]{:S(2)}) async-start(), calls=%async_computation.13 | async-start | bytes 3932160 | tf_op jit(solution)/shard_map/reduce_scatter | solution.py:379
  488.2 163.5 %reduce-scatter.14.cloned.1.call-start = ((), (), s32[]{:S(2)}) async-start(), calls=%async_computation.16 | async-start | bytes 5898240 | tf_op jit(solution)/shard_map/reduce_scatter | solution.py:351
  497.0 242.9 %reduce-scatter.12.cloned.1.call-start = ((), (), s32[]{:S(2)}) async-start(), calls=%async_computation.15 | async-start | bytes 5898240 | tf_op jit(solution)/shard_map/reduce_scatter | solution.py:352
  506.0 334.0 %reduce-scatter.10.cloned.1.call-start = ((), (), s32[]{:S(2)}) async-start(), calls=%async_computation.14 | async-start | bytes 5308416 | tf_op jit(solution)/shard_map/reduce_scatter | solution.py:398
  588.5 316.8 %all-gather.18.cloned.1.call-start = ((), (), s32[]{:S(2)}) async-start(), calls=%async_computation.18 | async-start | bytes 3932160 | tf_op jit(solution)/shard_map/all_gather | solution.py:356
  589.1 381.5 %all-gather.20.cloned.1.call-start = ((), (), s32[]{:S(2)}) async-start(), calls=%async_computation.19 | async-start | bytes 3932160 | tf_op jit(solution)/shard_map/all_gather | solution.py:391
  601.9 435.4 %all-reduce.4.cloned.1.call-start = ((), (), s32[]{:S(2)}) async-start(), calls=%async_computation.20 | async-start | bytes 5898240 | tf_op jit(solution)/shard_map/psum | solution.py:399
  604.4 3.2 copy-start.17
  609.6 3.2 copy-start.18
  614.8 3.1 copy-start.12
  617.9 222.1 %copy-start.14 = (s32[1280,256]{1,0:T(8,128)S(1)}, s32[1280,256]{1,0:T(8,128)}, u32[]{:S(2)}) copy-start(s32[1280,256]{1,0:T(8,128)} %copy-done.13) | copy-start | bytes 3932164
  860.3 88.1 %copy-start.37 = (f32[16,3]{0,1:T(4,128)S(1)}, f32[16,3]{0,1:T(4,128)}, u32[]{:S(2)}) copy-start(f32[16,3]{0,1:T(4,128)} %param.30) | copy-start | bytes 580
  860.3 88.1 %copy-start.42 = (f32[16,3]{0,1:T(4,128)S(1)}, f32[16,3]{0,1:T(4,128)}, u32[]{:S(2)}) copy-start(f32[16,3]{0,1:T(4,128)} %param.41) | copy-start | bytes 580
  860.3 88.1 %copy-start.43 = (f32[16,3]{0,1:T(4,128)S(1)}, f32[16,3]{0,1:T(4,128)}, u32[]{:S(2)}) copy-start(f32[16,3]{0,1:T(4,128)} %param.40) | copy-start | bytes 580
  860.3 88.7 %copy-start.33 = (f32[384,2]{0,1:T(2,128)S(1)}, f32[384,2]{0,1:T(2,128)}, u32[]{:S(2)}) copy-start(f32[384,2]{0,1:T(2,128)} %param.29) | copy-start | bytes 9220
  860.4 88.6 %copy-start.38 = (f32[384,2]{0,1:T(2,128)S(1)}, f32[384,2]{0,1:T(2,128)}, u32[]{:S(2)}) copy-start(f32[384,2]{0,1:T(2,128)} %param.39) | copy-start | bytes 9220
  860.4 88.6 %copy-start.39 = (f32[384,2]{0,1:T(2,128)S(1)}, f32[384,2]{0,1:T(2,128)}, u32[]{:S(2)}) copy-start(f32[384,2]{0,1:T(2,128)} %param.38) | copy-start | bytes 9220
  860.4 89.2 %copy-start.35 = (f32[384,2]{0,1:T(2,128)S(1)}, f32[384,2]{0,1:T(2,128)}, u32[]{:S(2)}) copy-start(f32[384,2]{0,1:T(2,128)} %param.31) | copy-start | bytes 9220
  860.4 89.2 %copy-start.40 = (f32[384,2]{0,1:T(2,128)S(1)}, f32[384,2]{0,1:T(2,128)}, u32[]{:S(2)}) copy-start(f32[384,2]{0,1:T(2,128)} %param.43) | copy-start | bytes 9220
  860.4 89.2 %copy-start.41 = (f32[384,2]{0,1:T(2,128)S(1)}, f32[384,2]{0,1:T(2,128)}, u32[]{:S(2)}) copy-start(f32[384,2]{0,1:T(2,128)} %param.42) | copy-start | bytes 9220
  970.5 66.8 %copy-start.7 = (f32[1,768,768]{1,2,0:T(8,128)S(1)}, f32[1,768,768]{1,2,0:T(8,128)}, u32[]{:S(2)}) copy-start(f32[1,768,768]{1,2,0:T(8,128)} %copy.272) | copy-start | bytes 7077892
  1047.4 3.2 copy-start.10
  1052.5 3.2 copy-start.9
  1057.7 3.2 copy-start.8
  1060.9 3.2 copy-start.15
  1064.4 3.4 copy-start.16
  (15 other events, 28.0 us)
Sparse Core Ops, SparseCore 0:
  10.7 83.1 all-gather.9
  102.9 44.5 all-gather.11
  149.6 89.4 all-gather.13
  241.1 87.8 all-gather.15
  487.8 35.8 reduce-scatter.5
  526.2 37.9 reduce-scatter.7
  566.5 85.2 reduce-scatter.13
  654.1 85.7 reduce-scatter.11
  744.1 95.8 reduce-scatter.9
  842.0 63.2 all-gather.17
  907.4 63.0 all-gather.19
  972.9 64.3 all-reduce.3

commit v2 on v1

--- a/solution.py
+++ b/solution.py
@@ -243,35 +243,57 @@
     capacity = max(4, 3 * block_len // (2 * expert_count))
     low = jnp.bfloat16
 
+    ctx_count = lax.axis_size("ctx")
+    pairs = [[i, i + 1] for i in range(0, ctx_count, 2)]
+    side = lax.rem(lax.axis_index("ctx"), 2)
     small_sizes = (local_rows * expert_count, local_rows * 2, table_rows * local_heads)
     small_count = sum(small_sizes)
-    small_rows = -(-small_count // model_width)
+    main_rows = 4 * local_width
+    pack_rows = -(-(main_rows + -(-small_count // local_rows)) // 32) * 32
+    small_room = (pack_rows - main_rows) * local_rows
+
+    def half(rows):
+        count = rows.shape[0] // 2
+        return lax.dynamic_slice_in_dim(rows, side * count, count, 0)
+
+    def pair_gather(rows, axis):
+        return lax.all_gather(rows, "ctx", axis=axis, axis_index_groups=pairs, tiled=True)
+
+    def pair_scatter(rows):
+        return lax.psum_scatter(
+            rows, "ctx", scatter_dimension=0, axis_index_groups=pairs, tiled=True
+        )
+
+    def ctx_sum(rows):
+        every = lax.all_gather(rows, "ctx", axis=0).astype(jnp.float32)
+        total = jnp.sum(every.reshape((ctx_count // 2, 2) + rows.shape), axis=0)
+        return total.reshape((2 * rows.shape[0],) + rows.shape[1:])
 
     def pack_small(router, gains, table):
-        flat = jnp.concatenate([router.reshape(-1), gains.reshape(-1), table.reshape(-1)])
-        flat = jnp.pad(flat, (0, small_rows * model_width - small_count))
-        return flat.reshape(small_rows, model_width)
+        lead = router.shape[:-2]
+        flat = jnp.concatenate([a.reshape(lead + (-1,)) for a in (router, gains, table)], axis=-1)
+        flat = jnp.pad(flat, [(0, 0)] * len(lead) + [(0, small_room - small_count)])
+        return flat.reshape(lead + (pack_rows - main_rows, local_rows))
 
     def cut_small(flat):
         ends = (small_sizes[0], small_sizes[0] + small_sizes[1])
         return flat[..., : ends[0]], flat[..., ends[0] : ends[1]], flat[..., ends[1] : small_count]
 
     main = jnp.concatenate([qkv_weight, out_weight[:, None, :]], axis=1)
-    main = jnp.transpose(main, (1, 2, 0)).astype(low).reshape(4 * local_width, local_rows)
-    shared = lax.all_gather(main, ("dp", "tp"), axis=0)
-    small = lax.all_gather(
-        pack_small(router_weight.astype(low), norm_gains.astype(low), bias_table.astype(low)),
-        ("dp", "tp"),
-        axis=0,
-    )
-    in_rows = lax.all_gather(expert_in[0].T.astype(low), "tp", axis=0, tiled=True)
-    down_rows = lax.all_gather(expert_down[0].astype(low), "tp", axis=0, tiled=True)
-
-    shared = shared.reshape(dp_count, tp_count, 4, local_width, local_rows)
+    main = jnp.transpose(main, (1, 2, 0)).astype(low).reshape(main_rows, local_rows)
+    small = pack_small(router_weight.astype(low), norm_gains.astype(low), bias_table.astype(low))
+    packed = half(jnp.concatenate([main, small], axis=0))
+    packed = pair_gather(lax.all_gather(packed, ("dp", "tp"), axis=0), 1)
+    in_half = lax.all_gather(half(expert_in[0].T.astype(low)), "tp", axis=0, tiled=True)
+    in_rows = pair_gather(in_half, 0)
+    down_half = lax.all_gather(half(expert_down[0].astype(low)), "tp", axis=0, tiled=True)
+    down_rows = pair_gather(down_half, 0)
+
+    shared = packed[:, :main_rows].reshape(dp_count, tp_count, 4, local_width, local_rows)
     shared = jnp.transpose(shared, (2, 1, 3, 0, 4)).reshape(4 * model_width, model_width)
     w_qkv = shared[: 3 * model_width]
     w_out = shared[3 * model_width :]
-    small = small.reshape(dp_count, tp_count, -1)
+    small = packed[:, main_rows:].reshape(dp_count, tp_count, -1)
     router_flat, gains_flat, table_flat = cut_small(small)
     w_router = router_flat[:, 0].reshape(model_width, expert_count)
     w_gains = gains_flat[:, 0].reshape(model_width, 2)
@@ -320,12 +342,25 @@
         target[None, :] == jnp.arange(expert_count * capacity, dtype=jnp.int32)[:, None]
     ).astype(low)
 
+    dp_place = lax.axis_index("dp")
+
     def to_experts(rows):
         slots = jnp.dot(dispatch_hot, rows, preferred_element_type=jnp.float32).astype(low)
-        return lax.all_to_all(slots, "dp", split_axis=0, concat_axis=0, tiled=True)
-
-    def from_experts(slots):
-        back = lax.all_to_all(slots.astype(low), "dp", split_axis=0, concat_axis=0, tiled=True)
+        if dp_count != 2:
+            return [lax.all_to_all(slots, "dp", split_axis=0, concat_axis=0, tiled=True)]
+        sent = lax.dynamic_slice_in_dim(slots, (1 - dp_place) * capacity, capacity, 0)
+        kept = lax.dynamic_slice_in_dim(slots, dp_place * capacity, capacity, 0)
+        return [kept, lax.ppermute(sent, "dp", [(0, 1), (1, 0)])]
+
+    def from_experts(parts):
+        parts = [part.astype(low) for part in parts]
+        if dp_count != 2:
+            back = lax.all_to_all(parts[0], "dp", split_axis=0, concat_axis=0, tiled=True)
+            return jnp.einsum("tr,td->rd", dispatch_hot, back, preferred_element_type=jnp.float32)
+        other = lax.ppermute(parts[1], "dp", [(0, 1), (1, 0)])
+        first = jnp.where(dp_place == 0, parts[0], other)
+        second = jnp.where(dp_place == 0, other, parts[0])
+        back = jnp.concatenate([first, second], axis=0)
         return jnp.einsum("tr,td->rd", dispatch_hot, back, preferred_element_type=jnp.float32)
 
     upstream = lax.dynamic_index_in_dim(cotangent, tp_place, 0, keepdims=False)
@@ -333,24 +368,31 @@
     row_grad = (gate_value[:, None] * upstream).astype(low)
     arrived = to_experts(normed_two_low)
     grad_arrived = to_experts(row_grad)
-    pre_act = jnp.einsum("md,fd->mf", arrived, in_rows, preferred_element_type=jnp.float32)
-    activated, gelu_back = jax.vjp(lambda a: jax.nn.gelu(a, approximate=True), pre_act)
-    active_low = activated.astype(low)
-    down_slots = jnp.dot(active_low, down_rows, preferred_element_type=jnp.float32)
-    expert_rows = from_experts(down_slots)
-    act_grad = jnp.einsum("md,fd->mf", grad_arrived, down_rows, preferred_element_type=jnp.float32)
-    pre_grad = gelu_back(act_grad)[0].astype(low)
-    slot_back = jnp.dot(pre_grad, in_rows, preferred_element_type=jnp.float32)
-    expert_backward_rows = from_experts(slot_back)
+    actives, downs, pre_grads, backs = [], [], [], []
+    for rows, grads in zip(arrived, grad_arrived):
+        pre_act = jnp.einsum("md,fd->mf", rows, in_rows, preferred_element_type=jnp.float32)
+        activated, gelu_back = jax.vjp(lambda a: jax.nn.gelu(a, approximate=True), pre_act)
+        active_low = activated.astype(low)
+        downs.append(jnp.dot(active_low, down_rows, preferred_element_type=jnp.float32))
+        act_grad = jnp.einsum("md,fd->mf", grads, down_rows, preferred_element_type=jnp.float32)
+        pre_grad = gelu_back(act_grad)[0].astype(low)
+        backs.append(jnp.dot(pre_grad, in_rows, preferred_element_type=jnp.float32))
+        actives.append(active_low)
+        pre_grads.append(pre_grad)
+    expert_rows = from_experts(downs)
+    expert_backward_rows = from_experts(backs)
     grad_down = jnp.einsum(
-        "mf,md->fd", active_low, grad_arrived, preferred_element_type=jnp.float32
+        "mf,md->fd",
+        jnp.concatenate(actives, axis=0),
+        jnp.concatenate(grad_arrived, axis=0),
+        preferred_element_type=jnp.float32,
     ).astype(low)
     grad_in = jnp.einsum(
-        "mf,md->fd", pre_grad, arrived, preferred_element_type=jnp.float32
-    ).astype(low)
-    grad_down = lax.psum_scatter(grad_down, "tp", scatter_dimension=0, tiled=True)
-    grad_in = lax.psum_scatter(grad_in, "tp", scatter_dimension=0, tiled=True)
-    grad_down, grad_in = lax.psum((grad_down, grad_in), "ctx")
+        "mf,md->fd",
+        jnp.concatenate(pre_grads, axis=0),
+        jnp.concatenate(arrived, axis=0),
+        preferred_element_type=jnp.float32,
+    ).astype(low)
 
     mixed_here = (hidden + gate_value[:, None] * expert_rows).astype(low)
     mixed_out = lax.all_gather(mixed_here, "tp", axis=0)
@@ -372,6 +414,10 @@
     heads_grad = jnp.einsum(
         "ro,co->rc", hidden_low, w_out, preferred_element_type=jnp.float32
     ).astype(low)
+    heads_grad, grad_down, grad_in = lax.optimization_barrier((heads_grad, grad_down, grad_in))
+    grad_down = lax.psum_scatter(pair_scatter(grad_down), "tp", scatter_dimension=0, tiled=True)
+    grad_in = lax.psum_scatter(pair_scatter(grad_in), "tp", scatter_dimension=0, tiled=True)
+    grad_down, grad_in = ctx_sum(grad_down), ctx_sum(grad_in)
     query_grad, key_grad, value_grad, strip_grad = run_backward(
         queries, heads_grad, key_value, bias, log_sums
     )
@@ -394,26 +440,32 @@
 
     main_grad = jnp.concatenate([grad_qkv, grad_out], axis=0).astype(low)
     main_grad = main_grad.reshape(4, tp_count, local_width, dp_count, local_rows)
-    main_grad = jnp.transpose(main_grad, (3, 1, 0, 2, 4)).reshape(-1, local_rows)
-    main_grad = lax.psum_scatter(main_grad, ("dp", "tp"), scatter_dimension=0, tiled=True)
-    main_grad = lax.psum(main_grad, "ctx").reshape(4, local_width, local_rows)
-    main_grad = jnp.transpose(main_grad, (2, 0, 1)).astype(jnp.float32)
-    small_grad = lax.psum(
-        jnp.concatenate([grad_router.reshape(-1), grad_gains.reshape(-1), grad_table.reshape(-1)]),
-        ("dp", "ctx", "tp"),
-    )
-    dp_place = lax.axis_index("dp")
-    ends = (model_width * expert_count, model_width * (expert_count + 2))
-    router_total = small_grad[: ends[0]].reshape(model_width, expert_count)
-    gains_total = small_grad[ends[0] : ends[1]].reshape(model_width, 2)
-    table_total = small_grad[ends[1] :].reshape(bucket_count, head_count)
-    router_total = lax.dynamic_slice_in_dim(router_total, dp_place * local_rows, local_rows, 0)
-    gains_total = lax.dynamic_slice_in_dim(gains_total, dp_place * local_rows, local_rows, 0)
-    table_total = lax.dynamic_slice(
-        table_total,
-        (dp_place * table_rows, tp_place * local_heads),
-        (table_rows, local_heads),
-    )
+    main_grad = jnp.transpose(main_grad, (3, 1, 0, 2, 4)).reshape(
+        dp_count, tp_count, main_rows, local_rows
+    )
+    owners = (dp_count, tp_count)
+
+    def by_rows(grad):
+        split = grad.reshape(dp_count, 1, local_rows, -1)
+        return jnp.broadcast_to(split, owners + split.shape[2:])
+
+    table_split = grad_table.reshape(dp_count, table_rows, tp_count, local_heads)
+    small_grad = pack_small(
+        by_rows(grad_router), by_rows(grad_gains), jnp.transpose(table_split, (0, 2, 1, 3))
+    ).astype(low)
+    packed_grad = jnp.concatenate([main_grad, small_grad], axis=2)
+    packed_grad = packed_grad.reshape(dp_count * tp_count, 2, pack_rows // 2, local_rows)
+    packed_grad = jnp.transpose(packed_grad, (1, 0, 2, 3)).reshape(-1, local_rows)
+    packed_grad = lax.psum_scatter(
+        pair_scatter(packed_grad), ("dp", "tp"), scatter_dimension=0, tiled=True
+    )
+    packed_grad = ctx_sum(packed_grad)
+    main_grad = packed_grad[:main_rows].reshape(4, local_width, local_rows)
+    main_grad = jnp.transpose(main_grad, (2, 0, 1))
+    router_total, gains_total, table_total = cut_small(packed_grad[main_rows:].reshape(-1))
+    router_total = router_total.reshape(local_rows, expert_count)
+    gains_total = gains_total.reshape(local_rows, 2)
+    table_total = table_total.reshape(table_rows, local_heads)
 
     qkv_new = adamw(qkv_weight, main_grad[:, :3], qkv_first, qkv_second, 2.0 * D ** (-0.5))
     out_new = adamw(
@@ -426,14 +478,14 @@
     gains_new = adamw(norm_gains, gains_total, gains_first, gains_second, 0.25)
     in_new = adamw(
         expert_in,
-        grad_in.T[None].astype(jnp.float32),
+        grad_in.T[None],
         in_first,
         in_second,
         2.0 * D ** (-0.5),
     )
     down_new = adamw(
         expert_down,
-        grad_down[None].astype(jnp.float32),
+        grad_down[None],
         down_first,
         down_second,
         2.0 * max(1, FF // (expert_count * expert_count)) ** (-0.5),

time: 1080 us -> 964 us (0.89)
  blocking collectives: 91.3 us -> 0 us
  matrix products: 116 us -> 104 us
    psum x1 -> x0, waiting for transfers between devices: 61.5 us -> none  [shards(): main_grad = lax.psum(main_grad, 'ctx').reshape(4, local_width, local_rows)]
    all_gather x1, waiting for transfers between devices: 20.3 us -> 64.2 us  [shards(): lax.all_gather((hidden_grad + input_back).astype(low), 'tp', axis=0)]
    reduce_scatter x3 -> x6, waiting for transfers between devices: 221 us -> 179 us  [the longest x1 67 us: shards(): lax.psum_scatter(pair_scatter(packed_grad), ('dp', 'tp'), scatter_dimensi...]
    psum x1 -> x0, blocking collectives: 41.4 us -> none  [shards(): lax.psum(jnp.concatenate([grad_router.reshape(-1), grad_gains.reshape(-1)...]
    all_gather x1 -> x0, blocking collectives: 32.6 us -> none  [shards(): lax.all_gather(pack_small(router_weight.astype(low), norm_gains.astype(lo...]
    all_gather x3 -> x9, waiting for transfers between devices: 174 us -> 206 us  [the longest x1 55.8 us: shards(): packed = pair_gather(lax.all_gather(packed, ('dp', 'tp'), axis=0), 1)]
    unnamed x118 -> x110, local copies, waits for them, and re-layouts: 46.2 us -> 16.3 us
    ppermute x0 -> x4, waiting for transfers between devices: none -> 29.1 us  [the longest x2 18.9 us: to_experts(): return [kept, lax.ppermute(sent, 'dp', [(0, 1), (1, 0)])]]
  transfers between devices with their start and end apart: 15 -> 24, of which waited for: 14 -> 19; matrix products, arithmetic and copies ran while one was open for 15% -> 19% of each run, Pallas kernels for 3% -> 3%
where the time goes in v2:
time: 964 us; the launch traced here: 956 us
  waiting for transfers between devices  599 us (62%)
  matrix products  104 us (11%)
  Pallas kernels  95.2 us (10%)
  local copies, waits for them, and re-layouts  91.8 us (10%)
  other arithmetic  44 us (5%)
  between operations  15.7 us (2%)
    reduce_scatter x1, waiting for transfers between devices, shards(): lax.psum_scatter(pair_scatter(packed_grad), ('dp', 'tp'), scatter_dimensi...  67 us
    all_gather x1, waiting for transfers between devices, shards(): mixed_out = lax.all_gather(mixed_here, 'tp', axis=0)  65 us
    all_gather x1, waiting for transfers between devices, shards(): lax.all_gather((hidden_grad + input_back).astype(low), 'tp', axis=0)  64.2 us
    pallas_call x1, Pallas kernels, run_backward(): pl.pallas_call(attend_backward, grid=(pairs, block_len // TILE), in_specs...  62.7 us
    all_gather x1, waiting for transfers between devices, shards(): packed = pair_gather(lax.all_gather(packed, ('dp', 'tp'), axis=0), 1)  55.8 us
    all_gather x3, waiting for transfers between devices, ctx_sum(): every = lax.all_gather(rows, 'ctx', axis=0).astype(jnp.float32)  51.7 us
    reduce_scatter x1, waiting for transfers between devices, shards(): lax.psum_scatter(pair_scatter(grad_in), 'tp', scatter_dimension=0, tiled=...  51.6 us
    reduce_scatter x1, waiting for transfers between devices, shards(): lax.psum_scatter(pair_scatter(grad_down), 'tp', scatter_dimension=0, tile...  49.7 us
  transfers between devices with their start and end apart: 24, of which 19 were waited for; matrix products, arithmetic and copies ran while one was open for 19% of the time, Pallas kernels for 3%

profile of v2, /device:TPU:0, one launch (start us, length us, event | category | flops | bytes accessed | tf_op | source)
XLA Modules:
  0.0 956.3 jit_solution(1229569993609747944)
XLA Ops:
  13.6 55.8 %all-gather.29.cloned.1.call-done = bf16[3200,384]{1,0:T(8,128)(2,1)} async-done(((bf16[400,384]{1,0:T(8,128)(2,1)}), bf16[3200,384]{1,0:T(8,128)(2,1)}) %all-gather.29.cloned.1.call-update) | async-done | bytes 2457616 | tf_op jit(solution)/shard_map/all_gather | solution.py:286
  75.5 8.7 all-gather.21.cloned.1.call-done
  86.3 2.8 slice.113
  94.6 2.6 convolution_convert_fusion.3
  97.3 40.7 %all-gather.25.cloned.1.call-done = bf16[1536,768]{0,1:T(8,128)(2,1)} async-done(((bf16[384,768]{0,1:T(8,128)(2,1)}), bf16[1536,768]{0,1:T(8,128)(2,1)}) %all-gather.25.cloned.1.call-update) | async-done | bytes 2359312 | tf_op jit(solution)/shard_map/all_gather | solution.py:287
  140.5 48.6 %all-gather.31.cloned.1.call-done = bf16[1,1536,768]{2,1,0:T(8,128)(2,1)} async-done(((bf16[1,384,768]{2,1,0:T(8,128)(2,1)}), bf16[1,1536,768]{2,1,0:T(8,128)(2,1)}) %all-gather.31.cloned.1.call-update) | async-done | bytes 2359312 | tf_op jit(solution)/shard_map/all_gather | solution.py:289
  189.8 2.9 fusion.164
  198.2 10.4 %fusion.1 = f32[12,1280,256]{2,0,1:T(8,128)} fusion(bf16[32,12,1]{0,1,2:T(8,128)(2,1)S(1)} %reshape.423, s32[1280,256]{1,0:T(8,128)S(1)} %select_add_fusion), kind=kOutput, calls=%fused_computation.2 | convolution fusion | flops 262144000 | bytes 17040128 | tf_op jit(solution)/shard_map/bh,bkq->hkq/dot_general | solution.py:312
  208.6 17.7 %copy.202.bias_ref = f32[12,1280,256]{2,1,0:T(8,128)} copy(f32[12,1280,256]{2,0,1:T(8,128)} %fusion.1) | data formatting | bytes 31457280 | tf_op jit(solution)/shard_map/bh,bkq->hkq/dot_general | solution.py:312
  228.3 8.1 all-gather.23.cloned.1.call-done.k_ref.v_ref
  236.4 2.8 copy-done.2
  239.2 32.5 %shard_map.407 = (bf16[512,768]{1,0:T(8,128)(2,1)S(1)}, f32[6,2,512]{2,1,0:T(2,128)S(1)}) custom-call(bf16[512,768]{1,0:T(8,128)(2,1)S(1)} %convolution_convert_fusion.6.q_ref, bf16[2048,1536]{1,0:T(8,128)(2,1)S(1)} %copy-done.2, bf16[2048,1536]{1,0:T(8,128)(2,1)S(1)} %copy-done.2, f32[12,1280,256]{2,1,0:T(8,128)} %copy.202.bias_ref), custom_call_target="tpu_custom_call" | custom-call | flops 12884901888 | bytes 20971520 | tf_op jit(solution)/shard_map/pallas_call | solution.py:155
  278.1 13.5 %collective-permute-done = bf16[384,768]{1,0:T(8,128)(2,1)} collective-permute-done((bf16[384,768]{1,0:T(8,128)(2,1)}, bf16[384,768]{1,0:T(8,128)(2,1)}, u32[]{:S(2)}, u32[]{:S(2)}) %collective-permute-start) | collective-permute-done | bytes 589856 | tf_op jit(solution)/shard_map/ppermute | solution.py:353
  291.6 8.3 multiply_convert_fusion
  299.9 5.2 fusion.68
  306.6 3.0 multiply_convert_fusion.1
  309.6 10.2 %collective-permute-done.1 = bf16[384,768]{1,0:T(8,128)(2,1)S(1)} collective-permute-done((bf16[384,768]{1,0:T(8,128)(2,1)S(1)}, bf16[384,768]{1,0:T(8,128)(2,1)S(1)}, u32[]{:S(2)}, u32[]{:S(2)}) %collective-permute-start.1) | collective-permute-done | bytes 589856 | tf_op jit(solution)/shard_map/ppermute | solution.py:360
  326.8 5.4 fusion.11
  333.7 5.3 collective-permute-done.2
  339.0 4.4 fusion.18
  343.4 2.9 convolution_convert_fusion.7
  347.8 6.0 convolution_convert_fusion.2
  353.8 8.6 convolution_convert_fusion.1
  362.5 5.3 broadcast_select_fusion.1
  369.3 2.7 convert_add_fusion
  373.1 62.7 %shard_map.408 = (bf16[512,768]{1,0:T(8,128)(2,1)S(1)}, bf16[2048,768]{1,0:T(8,128)(2,1)}, bf16[2048,768]{1,0:T(8,128)(2,1)}, f32[12,1280,256]{2,1,0:T(8,128)}) custom-call(bf16[512,768]{1,0:T(8,128)(2,1)S(1)} %convolution_convert_fusion.6.q_ref, bf16[512,768]{1,0:T(8,128)(2,1)S(1)} %convolution_convert_fusion.5.g_ref, ...), custom_call_target="tpu_custom_call" | custom-call | flops 32212254720 | bytes 41943040 | tf_op jit(solution)/shard_map/pallas_call | solution.py:180
  440.4 3.6 copy.205
  447.8 15.6 %fusion.95 = bf16[32,12]{0,1:T(8,128)(2,1)S(1)} fusion(f32[12,1280,256]{2,1,0:T(8,128)} %get-tuple-element.38, s32[1280,256]{1,0:T(8,128)} %copy-done.8), kind=kOutput, calls=%fused_computation.131 | convolution fusion | flops 262144000 | bytes 17040128 | tf_op jit(solution)/shard_map/hkq,bkq->bh/dot_general | solution.py:426
  467.4 5.6 reduce-scatter.9.cloned.1.call-done
  475.1 38.6 %reduce-scatter.11.cloned.1.call-done = bf16[512,768]{1,0:T(8,128)(2,1)} async-done(((bf16[2048,768]{1,0:T(8,128)(2,1)}), bf16[512,768]{1,0:T(8,128)(2,1)}) %reduce-scatter.11.cloned.1.call-update) | async-done | bytes 786448 | tf_op jit(solution)/shard_map/reduce_scatter | solution.py:425
  515.8 5.7 fusion.49
  522.2 4.0 convolution_convert_fusion
  528.7 10.3 %convert_element_type.275 = bf16[4,4,192,2,384]{4,3,2,1,0:T(2,128)(2,1)} reshape(bf16[3072,768]{1,0:T(8,128)(2,1)} %pad_maximum_fusion.1) | data formatting | bytes 9437184 | tf_op jit(solution)/shard_map/convert_element_type | solution.py:441
  539.0 4.2 copy.206
  543.7 2.7 copy.211
  551.0 10.5 %reduce-scatter.13.cloned.1.call-done = bf16[3200,384]{1,0:T(8,128)(2,1)} async-done(((bf16[6400,384]{1,0:T(8,128)(2,1)}), bf16[3200,384]{1,0:T(8,128)(2,1)}) %reduce-scatter.13.cloned.1.call-update) | async-done | bytes 2457616 | tf_op jit(solution)/shard_map/reduce_scatter | solution.py:263
  561.5 51.6 %reduce-scatter.19.cloned.1.call-done = bf16[384,768]{1,0:T(8,128)(2,1)} async-done(((bf16[1536,768]{1,0:T(8,128)(2,1)}), bf16[384,768]{1,0:T(8,128)(2,1)}) %reduce-scatter.19.cloned.1.call-update) | async-done | bytes 589840 | tf_op jit(solution)/shard_map/reduce_scatter | solution.py:419
  613.2 49.7 %reduce-scatter.23.cloned.1.call-done = bf16[384,768]{1,0:T(8,128)(2,1)} async-done(((bf16[1536,768]{1,0:T(8,128)(2,1)}), bf16[384,768]{1,0:T(8,128)(2,1)}) %reduce-scatter.23.cloned.1.call-update) | async-done | bytes 589840 | tf_op jit(solution)/shard_map/reduce_scatter | solution.py:418
  662.9 65.0 %all-gather.35.cloned.1.call-done = bf16[2048,768]{1,0:T(8,128)(2,1)} async-done(((bf16[512,768]{1,0:T(8,128)(2,1)}), bf16[2048,768]{1,0:T(8,128)(2,1)}) %all-gather.35.cloned.1.call-update) | async-done | bytes 3145744 | tf_op jit(solution)/shard_map/all_gather | solution.py:398
  727.8 64.2 %all-gather.37.cloned.1.call-done = bf16[2048,768]{1,0:T(8,128)(2,1)} async-done(((bf16[512,768]{1,0:T(8,128)(2,1)}), bf16[2048,768]{1,0:T(8,128)(2,1)}) %all-gather.37.cloned.1.call-update) | async-done | bytes 3145744 | tf_op jit(solution)/shard_map/all_gather | solution.py:437
  792.0 5.1 convert.46
  797.2 67.0 %reduce-scatter.15.cloned.1.call-done = bf16[400,384]{1,0:T(8,128)(2,1)} async-done(((bf16[3200,384]{1,0:T(8,128)(2,1)}), bf16[400,384]{1,0:T(8,128)(2,1)}) %reduce-scatter.15.cloned.1.call-update) | async-done | bytes 307216 | tf_op jit(solution)/shard_map/reduce_scatter | solution.py:459
  864.1 24.4 %all-gather.41.cloned.1.call-done = bf16[1536,768]{1,0:T(8,128)(2,1)} async-done(((bf16[384,768]{1,0:T(8,128)(2,1)}), bf16[1536,768]{1,0:T(8,128)(2,1)}) %all-gather.41.cloned.1.call-update) | async-done | bytes 2359312 | tf_op jit(solution)/shard_map/all_gather | solution.py:268
  888.5 3.7 convert_reduce_fusion.1
  894.3 20.0 %all-gather.43.cloned.1.call-done = bf16[1536,768]{1,0:T(8,128)(2,1)} async-done(((bf16[384,768]{1,0:T(8,128)(2,1)}), bf16[1536,768]{1,0:T(8,128)(2,1)}) %all-gather.43.cloned.1.call-update) | async-done | bytes 2359312 | tf_op jit(solution)/shard_map/all_gather | solution.py:268
  917.3 8.7 multiply_subtract_fusion
  926.0 7.4 all-gather.39.cloned.1.call-done
  936.3 4.3 slice.107
  (258 shorter events, 91.8 us)
Async XLA Ops:
  7.2 130.8 %copy-start = (s32[4,512,1]{1,2,0:T(1,128)S(1)}, s32[4,512,1]{1,2,0:T(1,128)}, u32[]{:S(2)}) copy-start(s32[4,512,1]{1,2,0:T(1,128)} %param.26) | copy-start | bytes 24580
  7.2 62.2 %all-gather.29.cloned.1.call-start = ((), (), s32[]{:S(2)}) async-start(), calls=%async_computation.20 | async-start | bytes 2764800 | tf_op jit(solution)/shard_map/all_gather | solution.py:286
  13.6 70.7 %all-gather.21.cloned.1.call-start = ((), (), s32[]{:S(2)}) async-start(), calls=%async_computation.8 | async-start | bytes 7372800 | tf_op jit(solution)/shard_map/all_gather | solution.py:260
  69.4 4.7 copy-start.20
  69.4 68.5 %all-gather.25.cloned.1.call-start = ((), (), s32[]{:S(2)}) async-start(), calls=%async_computation.10 | async-start | bytes 2949120 | tf_op jit(solution)/shard_map/all_gather | solution.py:287
  71.8 117.4 %all-gather.31.cloned.1.call-start = ((), (), s32[]{:S(2)}) async-start(), calls=%async_computation.21 | async-start | bytes 2949120 | tf_op jit(solution)/shard_map/all_gather | solution.py:289
  74.1 162.3 %all-gather.23.cloned.1.call-start = ((), (), s32[]{:S(2)}) async-start(), calls=%async_computation.9 | async-start | bytes 7864320 | tf_op jit(solution)/shard_map/all_gather | solution.py:321
  85.3 104.4 %copy-start.22 = (bf16[2,4,12288]{2,1,0:T(4,128)(2,1)}, bf16[2,4,12288]{2,1,0:T(4,128)(2,1)S(1)}, u32[]{:S(2)}) copy-start(bf16[2,4,12288]{2,1,0:T(4,128)(2,1)S(1)} %reshape.371) | copy-start | bytes 589828
  94.6 131.7 %copy-start.26 = (f32[768]{0:T(1024)}, f32[768]{0:T(1024)S(1)}, u32[]{:S(2)}) copy-start(f32[768]{0:T(1024)S(1)} %get-tuple-element.117) | copy-start | bytes 9220
  97.2 180.8 %all-gather.27.cloned.1.call-start = ((), (), s32[]{:S(2)}) async-start(), calls=%async_computation.11 | async-start | bytes 7077888 | tf_op jit(solution)/shard_map/all_gather | solution.py:260
  138.0 161.9 %all-gather.33.cloned.1.call-start = ((), (), s32[]{:S(2)}) async-start(), calls=%async_computation.22 | async-start | bytes 7077888 | tf_op jit(solution)/shard_map/all_gather | solution.py:260
  140.5 57.7 %copy-start.8 = (s32[1280,256]{1,0:T(8,128)}, s32[1280,256]{1,0:T(8,128)S(1)}, u32[]{:S(2)}) copy-start(s32[1280,256]{1,0:T(8,128)S(1)} %select_add_fusion) | copy-start | bytes 3932164
  189.2 283.8 %reduce-scatter.9.cloned.1.call-start = ((), (), s32[]{:S(2)}) async-start(), calls=%async_computation.12 | async-start | bytes 3932160 | tf_op jit(solution)/shard_map/reduce_scatter | solution.py:424
  208.6 17.7 %copy-start.32 = (f32[512]{0:T(512)S(1)}, f32[512]{0:T(512)}, u32[]{:S(2)}) copy-start(f32[512]{0:T(512)} %fusion.149) | copy-start | bytes 6148
  239.2 32.5 %copy-start.15 = (bf16[96,8,2,384]{3,1,2,0:T(8,128)(2,1)S(1)}, bf16[96,8,2,384]{3,1,2,0:T(8,128)(2,1)}, u32[]{:S(2)}) copy-start(bf16[96,8,2,384]{3,1,2,0:T(8,128)(2,1)} %copy.223) | copy-start | bytes 3538948
  274.0 3.3 copy-start.28
  275.8 15.8 %collective-permute-start = (bf16[384,768]{1,0:T(8,128)(2,1)}, bf16[384,768]{1,0:T(8,128)(2,1)}, u32[]{:S(2)}, u32[]{:S(2)}) collective-permute-start(bf16[384,768]{1,0:T(8,128)(2,1)} %get-tuple-element.155), channel_id=1, source_target_pairs={{0,16},{16,0},{1,17},{17,1},{2,18},{18,2},{3,19},{19,3},{4,20},{20... | collective-permute-start | bytes 1769480 | tf_op jit(solution)/shard_map/ppermute | solution.py:353
  299.9 6.7 copy-start.45
  305.1 14.7 %collective-permute-start.1 = (bf16[384,768]{1,0:T(8,128)(2,1)S(1)}, bf16[384,768]{1,0:T(8,128)(2,1)S(1)}, u32[]{:S(2)}, u32[]{:S(2)}) collective-permute-start(bf16[384,768]{1,0:T(8,128)(2,1)S(1)} %fusion.68), channel_id=1, source_target_pairs={{0,16},{16,0},{1,17},{17,1},{2,18},{18,2},{3,19},{19,3},{4,20},{20... | collective-permute-start | bytes 1769480 | tf_op jit(solution)/shard_map/ppermute | solution.py:360
  306.6 13.2 %copy-start.46 = (bf16[1,3072,768]{2,1,0:T(8,128)(2,1)S(1)}, bf16[1,3072,768]{2,1,0:T(8,128)(2,1)}, u32[]{:S(2)}) copy-start(bf16[1,3072,768]{2,1,0:T(8,128)(2,1)} %all-gather.33.cloned.1.call-done) | copy-start | bytes 14155780
  325.1 13.9 %slice-start.1 = ((s8[4718592]{0:T(1024)(128)(4,1)}), s8[4194304]{0:T(1024)(128)(4,1)S(1)}, s32[]{:S(2)}) async-start(s8[4718592]{0:T(1024)(128)(4,1)} %bitcast.233), calls=%async_computation.29 | async-start | bytes 8388608
  325.2 13.8 %collective-permute-start.2 = (bf16[384,768]{1,0:T(8,128)(2,1)S(1)}, bf16[384,768]{1,0:T(8,128)(2,1)S(1)}, u32[]{:S(2)}, u32[]{:S(2)}) collective-permute-start(bf16[384,768]{1,0:T(8,128)(2,1)S(1)} %get-tuple-element.151), channel_id=1, source_target_pairs={{0,16},{16,0},{1,17},{17,1},{2,18},{18,2},{3,19},{19,3},{4,20},{20... | collective-permute-start | bytes 1769480 | tf_op jit(solution)/shard_map/ppermute | solution.py:353
  326.7 12.3 %slice-start.2 = ((s8[4718592]{0:T(1024)(128)(4,1)}), s8[524288]{0:T(1024)(128)(4,1)S(1)}, s32[]{:S(2)}) async-start(s8[4718592]{0:T(1024)(128)(4,1)} %bitcast.233), calls=%async_computation.30 | async-start | bytes 1048576
  343.4 4.4 copy-start.48
  346.4 16.1 %collective-permute-start.3 = (bf16[384,768]{1,0:T(8,128)(2,1)}, bf16[384,768]{1,0:T(8,128)(2,1)}, u32[]{:S(2)}, u32[]{:S(2)}) collective-permute-start(bf16[384,768]{1,0:T(8,128)(2,1)} %convolution_convert_fusion.7), channel_id=1, source_target_pairs={{0,16},{16,0},{1,17},{17,1},{2,18},{18,2},{3,19},{19,3},{4,20},{20... | collective-permute-start | bytes 1769480 | tf_op jit(solution)/shard_map/ppermute | solution.py:360
  362.5 5.4 copy-start.7
  362.5 5.4 copy-start.13
  435.8 77.9 %reduce-scatter.11.cloned.1.call-start = ((), (), s32[]{:S(2)}) async-start(), calls=%async_computation.13 | async-start | bytes 3932160 | tf_op jit(solution)/shard_map/reduce_scatter | solution.py:425
  436.5 110.0 %reduce-scatter.17.cloned.1.call-start = ((), (), s32[]{:S(2)}) async-start(), calls=%async_computation.16 | async-start | bytes 7077888 | tf_op jit(solution)/shard_map/reduce_scatter | solution.py:263
  437.1 110.1 %reduce-scatter.21.cloned.1.call-start = ((), (), s32[]{:S(2)}) async-start(), calls=%async_computation.18 | async-start | bytes 7077888 | tf_op jit(solution)/shard_map/reduce_scatter | solution.py:263
  437.9 123.6 %reduce-scatter.13.cloned.1.call-start = ((), (), s32[]{:S(2)}) async-start(), calls=%async_computation.14 | async-start | bytes 7372800 | tf_op jit(solution)/shard_map/reduce_scatter | solution.py:263
  467.4 48.3 %copy-start.27 = (f32[768]{0:T(1024)S(1)}, f32[768]{0:T(1024)}, u32[]{:S(2)}) copy-start(f32[768]{0:T(1024)} %copy-done.26) | copy-start | bytes 9220
  467.4 48.3 %copy-start.33 = (f32[512]{0:T(512)S(1)}, f32[512]{0:T(512)}, u32[]{:S(2)}) copy-start(f32[512]{0:T(512)} %fusion.149) | copy-start | bytes 6148
  515.7 5.7 copy-start.37
  515.7 6.2 copy-start.34
  546.4 66.7 %reduce-scatter.19.cloned.1.call-start = ((), (), s32[]{:S(2)}) async-start(), calls=%async_computation.17 | async-start | bytes 2949120 | tf_op jit(solution)/shard_map/reduce_scatter | solution.py:419
  547.2 115.6 %reduce-scatter.23.cloned.1.call-start = ((), (), s32[]{:S(2)}) async-start(), calls=%async_computation.19 | async-start | bytes 2949120 | tf_op jit(solution)/shard_map/reduce_scatter | solution.py:418
  547.8 180.1 %all-gather.35.cloned.1.call-start = ((), (), s32[]{:S(2)}) async-start(), calls=%async_computation.23 | async-start | bytes 3932160 | tf_op jit(solution)/shard_map/all_gather | solution.py:398
  548.4 243.7 %all-gather.37.cloned.1.call-start = ((), (), s32[]{:S(2)}) async-start(), calls=%async_computation.24 | async-start | bytes 3932160 | tf_op jit(solution)/shard_map/all_gather | solution.py:437
  551.0 313.2 %reduce-scatter.15.cloned.1.call-start = ((), (), s32[]{:S(2)}) async-start(), calls=%async_computation.15 | async-start | bytes 2764800 | tf_op jit(solution)/shard_map/reduce_scatter | solution.py:459
  561.5 327.0 %all-gather.41.cloned.1.call-start = ((), (), s32[]{:S(2)}) async-start(), calls=%async_computation.26 | async-start | bytes 2949120 | tf_op jit(solution)/shard_map/all_gather | solution.py:268
  613.1 301.1 %all-gather.43.cloned.1.call-start = ((), (), s32[]{:S(2)}) async-start(), calls=%async_computation.27 | async-start | bytes 2949120 | tf_op jit(solution)/shard_map/all_gather | solution.py:268
  662.8 270.5 %all-gather.39.cloned.1.call-start = ((), (), s32[]{:S(2)}) async-start(), calls=%async_computation.25 | async-start | bytes 1536000 | tf_op jit(solution)/shard_map/all_gather | solution.py:268
  935.6 6.3 copy-start.17
  936.0 8.0 copy-start.11
  936.0 8.0 copy-start.18
  936.3 5.6 copy-start.21
  944.2 3.2 copy-start.12
  (28 other events, 59.6 us)
Sparse Core Ops, SparseCore 0:
  13.7 55.6 all-gather.28
  70.9 13.2 all-gather.20
  86.4 51.4 all-gather.24
  140.0 49.1 all-gather.30
  191.2 45.1 all-gather.22
  237.8 14.4 all-gather.26
  253.8 15.6 all-gather.32
  435.9 37.0 reduce-scatter.8
  475.7 37.9 reduce-scatter.10
  515.8 12.6 reduce-scatter.16
  530.9 13.7 reduce-scatter.20
  547.5 13.9 reduce-scatter.12
  563.8 49.2 reduce-scatter.18
  615.3 47.5 reduce-scatter.22
  664.8 62.9 all-gather.34
  729.8 62.1 all-gather.36
  795.5 68.5 reduce-scatter.14
  865.5 22.9 all-gather.40
  890.1 24.0 all-gather.42
  915.6 17.7 all-gather.38
